TPU v7x, 256 devices: a whole 4x4x8 slice. The times are simulated.
256 devices in a mesh: tm: 8 (over x, core), node: 32 (over z, y).
Axes of the slice: x: 4, y: 4, z: 8, core: 2. Of those that a mesh axis runs over, the one named last changes fastest.
Arguments:
- memory: float32 [16384, 256], P('node'), may hold values from -6 to 6
- touched: int32 [8, 32, 256], P(None, 'node'), may hold values from 0 to 511, as said below
- src_slot: int32 [8, 32, 512], P('tm', 'node'), may hold values from 0 to 255, as said below
- ev_count: int32 [8, 32], P('tm', 'node'), may hold values from 256 to 512, as said below
- serve_rows: int32 [8, 32, 1024], P('tm', 'node'), may hold values from 0 to 511
- dst_slot: int32 [8, 32, 512], P('tm', 'node'), may hold values from 0 to 1023
- nbr_slot: int32 [8, 32, 10, 512], P('tm', 'node'), may hold values from 0 to 1023
- ev_gap: int32 [8, 32, 512], P('tm', 'node'), may hold values from 0 to 999
- nbr_gap: int32 [8, 32, 10, 512], P('tm', 'node'), may hold values from 1 to 999
- time_freq: float32 [100], replicated, may hold values from 0.001 to 0.1
- time_phase: float32 [100], replicated, may hold values from -3.140625 to 3.140625
- w_msg: bfloat16 [612, 256], replicated, may hold values from -0.25 to 0.25
- w_in: bfloat16 [256, 768], replicated, may hold values from -0.375 to 0.375
- w_hid: bfloat16 [256, 768], replicated, may hold values from -0.375 to 0.375
- w_nbr: bfloat16 [356, 256], replicated, may hold values from -0.09375 to 0.09375
- w_out: bfloat16 [512, 256], replicated, may hold values from -0.25 to 0.25
Outputs:
- embeddings: bfloat16 [8, 32, 512, 256], P('tm', 'node')
- memory_after: float32 [8, 16384, 256], P('tm', 'node')
Inputs may be any that keep to these rules, and one draw needn't show every extreme that they name: `touched`: for every segment and shard the 256 rows are distinct local rows. `src_slot`: the first 256 events of each segment and shard name every touched position exactly once. `ev_count`: in every segment some shard has all 512 event slots live.
All inputs are finite; a program needn't handle non-finite values.
Results may differ from a plain program's by a relative error of at most 0.015.
Values may be sent and summed in bfloat16 or wider, within the bound.
No kernel may reach another device: no remote copies, remote signals or barrier semaphores. Data moves between devices by JAX's collectives and lax.ppermute only.
A program may use at most 128 MiB of HBM per device.

v0:
```python
import functools

import jax
import jax.numpy as jnp
from jax import lax
from jax.experimental import pallas as pl
from jax.experimental.pallas import tpu as pltpu
from jax.sharding import PartitionSpec as P

DM = 256
TD = 100
CODE = 128
GAPS = 1024
NBRS = 10
F32 = jnp.float32
BF16 = jnp.bfloat16
VMEM = pl.BlockSpec(memory_space=pltpu.VMEM)
SMEM = pl.BlockSpec(memory_space=pltpu.SMEM)
ANY = pl.BlockSpec(memory_space=pl.ANY)
HBM = pl.BlockSpec(memory_space=pltpu.HBM)


def dot(a, b):
    return jnp.dot(a, b, preferred_element_type=F32)


def dot_nt(a, b):
    return lax.dot_general(a, b, (((1,), (1,)), ((), ())), preferred_element_type=F32)


def iota(shape, axis):
    return lax.broadcasted_iota(jnp.int32, shape, axis)


def ones_where(mask):
    return jnp.where(mask, 1.0, 0.0).astype(BF16)


def same16(a, b):
    mask = a.astype(jnp.int16) == b.astype(jnp.int16)
    return jnp.where(mask, jnp.ones((), BF16), jnp.zeros((), BF16))


def pick_rows(height, row):
    row = row.astype(jnp.int16)
    base = iota((16, row.shape[1]), 0).astype(jnp.int16)
    one, zero = jnp.ones((), BF16), jnp.zeros((), BF16)
    return jnp.concatenate(
        [jnp.where(base + jnp.int16(i) == row, one, zero) for i in range(0, height, 16)], axis=0
    )


def split_two(x):
    high = x.astype(BF16)
    return high, (x - high.astype(F32)).astype(BF16)


def hit_rows(place):
    return jnp.max(place.astype(F32), axis=1, keepdims=True) > 0.5


def copies(pairs, sems):
    return [pltpu.make_async_copy(src, dst, sems.at[i]) for i, (src, dst) in enumerate(pairs)]


def pack_kernel(serve_ref, dst_ref, src_ref, gap_ref, count_ref, out_ref, scr, in_sems, out_sems):
    at, pairs = 0, []
    for ref in (serve_ref, dst_ref, src_ref, gap_ref):
        pairs.append((ref, scr.at[at : at + ref.shape[0]]))
        at += ref.shape[0]
    loads = copies(pairs, in_sems)
    for copy in loads:
        copy.start()
    scr[at:, :] = jnp.full((scr.shape[0] - at, 128), count_ref[0, 0], jnp.int32)
    for copy in loads:
        copy.wait()
    sends = copies([(scr, out_ref.at[i]) for i in range(out_ref.shape[0])], out_sems)
    for copy in sends:
        copy.start()
    for copy in sends:
        copy.wait()


def first_serve_kernel(serve_ref, memory_ref, *rest):
    served_out, memory_out = rest[-2:]
    memory = memory_ref[...].astype(BF16)
    memory_out[...] = memory
    pick = same16(serve_ref[:, 0:1], iota((serve_ref.shape[0], memory.shape[0]), 1))
    served_out[...] = dot(pick, memory).astype(BF16)


def table_kernel(freq_ref, phase_ref, high_out, low_out):
    gap = iota(high_out.shape, 0).astype(F32)
    high, low = split_two(jnp.cos(gap * freq_ref[...] + phase_ref[...]))
    high_out[...] = high
    low_out[...] = low


def links_kernel(src_ref, dst_ref, gap_ref, count_ref, table_ref, w_code_ref, links_out, code_out, inv_out):
    turn = pl.program_id(0)
    touch, slots = links_out.shape[1:]
    events = src_ref.shape[1]
    row = pl.ds(turn, 1)
    live = iota((touch, events), 1) < count_ref[turn]
    member_mask = jnp.logical_and(iota((touch, events), 0) == src_ref[row, :], live)
    member_f = jnp.where(member_mask, 1.0, 0.0)
    member = member_f.astype(BF16)
    inv = 1.0 / jnp.sum(member_f, axis=1, keepdims=True)
    inv_out[0] = jnp.broadcast_to(inv, inv_out.shape[1:])
    dst_pick = pick_rows(slots, dst_ref[row, :])
    links_out[0] = dot_nt(member, dst_pick).astype(BF16)
    gap_pick = pick_rows(table_ref.shape[0], gap_ref[row, :])
    gap_count = dot_nt(member, gap_pick).astype(BF16)
    code_mean = (dot(gap_count, table_ref[...]) * inv).astype(BF16)
    code_out[0] = dot(code_mean, w_code_ref[2 * DM :, :]).astype(BF16)


def ready_kernel(
    turn,
    last,
    me_ref,
    own_ref,
    kept_ref,
    fresh_ref,
    touched_ref,
    touched_t_ref,
    serve_t_ref,
    w_msg_ref,
    w_hid_ref,
    links_ref,
    code_ref,
    inv_ref,
    *rest,
):
    outs = rest[turn > 1 : (turn > 1) + 9]
    total_out, inv_out, links_out, base_out, gh_out, held_out, static_out, hits_out, kept_out = outs
    links_scr, code_scr, memory_scr, sems, snap_sem = rest[-5:]
    rows, touch, half = kept_ref.shape[0], touched_ref.shape[1], own_ref.shape[0]
    loads = copies(
        [
            (links_ref.at[turn, :, :half], links_scr),
            (links_ref.at[turn, :, half:], links_out),
            (code_ref.at[turn], code_scr),
            (inv_ref.at[turn], inv_out),
        ],
        sems,
    )
    for copy in loads:
        copy.start()
    memory = kept_ref[...]
    if turn > 0:
        place = pick_rows(rows, touched_ref[turn - 1 : turn, :])
        memory = memory + dot(place, fresh_ref[...]).astype(BF16)
        snap_store = pltpu.make_async_copy(memory_scr, rest[-6], snap_sem)

        @pl.when(me_ref[0] == turn - 1)
        def _():
            memory_scr[...] = memory.astype(F32)
            snap_store.start()

    pick = same16(touched_t_ref[:, turn : turn + 1], iota((touch, rows), 1))
    held = dot(pick, memory).astype(BF16)
    held_out[...] = held
    gh_out[...] = dot(held, w_hid_ref[...])
    base = dot(held, w_msg_ref[:DM, :])
    now = touched_ref[turn : turn + 1, :]
    hit = dot(pick_rows(rows, now), jnp.ones((touch, 128), BF16))
    free = (1.0 - hit).astype(BF16)
    kept = memory * jnp.concatenate([free, free], axis=1)
    kept_out[...] = kept
    if not last:
        wanted = serve_t_ref[:, turn + 1 : turn + 2]
        serve = same16(wanted, iota((half, rows), 1))
        static_out[...] = dot(serve, kept).astype(BF16)
        hits_out[...] = same16(wanted, now)
    loads[0].wait()
    total_out[...] = dot(links_scr[...], own_ref[...])
    loads[2].wait()
    base_out[...] = base + code_scr[...].astype(F32)
    loads[1].wait()
    loads[3].wait()
    if turn > 0:

        @pl.when(me_ref[0] == turn - 1)
        def _():
            snap_store.wait()


def updated(other, total, inv, links, base, gh, held, w_dst, w_in):
    raw = total + dot(links, other)
    raw = (raw * jnp.concatenate([inv, inv], axis=1)).astype(BF16)
    aggregate = (dot(raw, w_dst) + base).astype(BF16)
    gi = dot(aggregate, w_in)
    reset_gate = jax.nn.sigmoid(gi[:, :DM] + gh[:, :DM])
    update_gate = jax.nn.sigmoid(gi[:, DM : 2 * DM] + gh[:, DM : 2 * DM])
    candidate = jnp.tanh(gi[:, 2 * DM :] + reset_gate * gh[:, 2 * DM :])
    return (1.0 - update_gate) * candidate + update_gate * held.astype(F32)


def update_kernel(
    turn,
    me_ref,
    own_ref,
    other_ref,
    total_ref,
    inv_ref,
    links_ref,
    base_ref,
    gh_ref,
    held_ref,
    static_ref,
    hits_ref,
    w_msg_ref,
    w_in_ref,
    *rest,
):
    fresh_out, served_out, kept_out, fresh_kept_out, kept_sems = rest[-5:]
    half = own_ref.shape[0]
    mine = me_ref[0] == turn
    keeps = copies(
        [
            (own_ref, kept_out.at[:half]),
            (other_ref, kept_out.at[half:]),
            (fresh_out, fresh_kept_out),
        ],
        kept_sems,
    )

    @pl.when(mine)
    def _():
        for copy in keeps[:2]:
            copy.start()

    fresh = updated(
        other_ref[...],
        total_ref[...],
        inv_ref[...],
        links_ref[...],
        base_ref[...],
        gh_ref[...],
        held_ref[...],
        w_msg_ref[DM : 2 * DM, :],
        w_in_ref[...],
    )
    fresh_b = fresh.astype(BF16)
    fresh_out[...] = fresh_b

    @pl.when(mine)
    def _():
        keeps[2].start()

    served = dot(hits_ref[...], fresh_b) + static_ref[...].astype(F32)
    served_out[...] = served.astype(BF16)

    @pl.when(mine)
    def _():
        for copy in keeps:
            copy.wait()


def embedded(live_count, nbr, kept, codes, src_t, fresh_b, w_nbr, w_nbr_code, w_out):
    events = src_t.shape[0]
    near = dot(nbr, kept)
    hidden = dot(near.astype(BF16), w_nbr) + dot(codes, w_nbr_code)
    hidden = jnp.maximum(hidden, 0.0).astype(BF16)
    src_pick = same16(src_t, iota((events, fresh_b.shape[0]), 1))
    src_new = dot(src_pick, fresh_b).astype(BF16)
    out = dot(src_new, w_out[:DM, :]) + dot(hidden, w_out[DM:, :])
    live = iota((events, 1), 0) < live_count
    return jnp.where(live, out, 0.0).astype(BF16)


def last_kernel(
    turn,
    me_ref,
    counts_ref,
    own_ref,
    other_ref,
    total_ref,
    inv_ref,
    links_ref,
    base_ref,
    gh_ref,
    held_ref,
    memory_ref,
    w_msg_ref,
    w_in_ref,
    touched_ref,
    nbr_ref,
    codes_ref,
    lists_ref,
    w_nbr_ref,
    w_out_ref,
    rows_ref,
    fresh_kept_ref,
    snap_in_ref,
    emb_out,
    snap_out,
    rows_scr,
    fresh_scr,
    snap_scr,
    emb_scr,
    rows_sems,
    out_sems,
):
    mine = me_ref[0] == turn
    half = own_ref.shape[0]
    early = copies([(rows_ref, rows_scr), (fresh_kept_ref, fresh_scr)], rows_sems)
    snap_store = pltpu.make_async_copy(snap_scr, snap_out, out_sems.at[0])

    @pl.when(jnp.logical_not(mine))
    def _():
        for copy in early:
            copy.start()
        for copy in early:
            copy.wait()

    @pl.when(mine)
    def _():
        rows_scr[:half, :] = own_ref[...]
        rows_scr[half:, :] = other_ref[...]
        fresh = updated(
            other_ref[...],
            total_ref[...],
            inv_ref[...],
            links_ref[...],
            base_ref[...],
            gh_ref[...],
            held_ref[...],
            w_msg_ref[DM : 2 * DM, :],
            w_in_ref[...],
        )
        fresh_scr[...] = fresh.astype(BF16)
        rows, touch = memory_ref.shape[0], touched_ref.shape[1]
        place = pick_rows(rows, touched_ref[turn : turn + 1, :])
        high, low = split_two(fresh)
        snap_scr[...] = memory_ref[...].astype(F32) + (dot(place, high) + dot(place, low))
        snap_store.start()

    emb_scr[...] = embedded(
        counts_ref[me_ref[0]],
        nbr_ref[...],
        rows_scr[...],
        codes_ref[...],
        lists_ref[:, 2 * NBRS : 2 * NBRS + 1],
        fresh_scr[...],
        w_nbr_ref[:DM, :],
        w_nbr_ref[DM:, :],
        w_out_ref,
    )
    store_emb = pltpu.make_async_copy(emb_scr, emb_out, out_sems.at[1])
    store_emb.start()

    @pl.when(mine)
    def _():
        snap_store.wait()

    store_emb.wait()


def count_block(lists, number, begin, width):
    lanes = iota((lists.shape[0], width), 1)
    total = same16(lists[:, begin : begin + 1], lanes)
    for q in range(begin + 1, begin + number):
        total += same16(lists[:, q : q + 1], lanes)
    return total


def neighbours_kernel(after_ref, lists_ref, out_ref):
    block = 64

    def step(i, carry):
        at = pl.ds(pl.multiple_of(i * block, block), block)
        out_ref[at, :] = count_block(lists_ref[at, :], NBRS, 0, out_ref.shape[1])
        return carry

    lax.fori_loop(0, out_ref.shape[0] // block, step, 0)


def codes_kernel(after_ref, lists_ref, high_ref, low_ref, out_ref):
    block = 128

    def step(i, carry):
        at = pl.ds(pl.multiple_of(i * block, block), block)
        counts = count_block(lists_ref[at, :], NBRS, NBRS, high_ref.shape[0])
        out_ref[at, :] = (dot(counts, high_ref[...]) + dot(counts, low_ref[...])).astype(BF16)
        return carry

    lax.fori_loop(0, out_ref.shape[0] // block, step, 0)


def tie_kernel(*refs):
    pass


def in_hbm(dims, dtype):
    return pltpu.HBM(dims, dtype)


def stay(arrays):
    return [pltpu.with_memory_space_constraint(x, pltpu.HBM) for x in arrays]


def shape(dims, dtype):
    return jax.ShapeDtypeStruct(dims, dtype)


def params(mib=16):
    return pltpu.CompilerParams(vmem_limit_bytes=mib * 1024 * 1024)


def cost(flops, bytes_accessed):
    return pl.CostEstimate(flops=flops, bytes_accessed=bytes_accessed, transcendentals=0)


def body(
    memory,
    touched,
    src_slot,
    ev_count,
    serve_rows,
    dst_slot,
    nbr_slot,
    ev_gap,
    nbr_gap,
    time_freq,
    time_phase,
    w_msg,
    w_in,
    w_hid,
    w_nbr,
    w_out,
):
    me = lax.axis_index("tm")
    core = me % 2
    sections = lax.axis_size("tm")
    shards = lax.axis_size("node")
    rows = memory.shape[0]
    events = src_slot.shape[2]
    slots = serve_rows.shape[2]
    half = slots // 2
    capacity = slots // shards
    part = capacity // 2
    touched = touched[:, 0, :]
    touch = touched.shape[1]

    lists = [
        serve_rows.reshape(-1, 128),
        dst_slot.reshape(-1, 128),
        src_slot.reshape(-1, 128),
        ev_gap.reshape(-1, 128),
    ]
    lines = sum(x.shape[0] for x in lists) + 4
    packed = pl.pallas_call(
        pack_kernel,
        out_shape=shape((sections, lines, 128), jnp.int32),
        in_specs=[HBM] * 4 + [SMEM],
        out_specs=HBM,
        scratch_shapes=[
            pltpu.VMEM((lines, 128), jnp.int32),
            pltpu.SemaphoreType.DMA((4,)),
            pltpu.SemaphoreType.DMA((sections,)),
        ],
        compiler_params=params(),
        name="pack",
    )(*stay(lists), ev_count)
    everyone = lax.all_to_all(packed, "tm", split_axis=0, concat_axis=0, tiled=True).reshape(
        sections, -1
    )
    serve_all = everyone[:, :slots].reshape(sections, shards, 2, part)
    serve_own = jnp.where(core == 0, serve_all[:, :, 0], serve_all[:, :, 1])
    serve_t = serve_own.reshape(sections, half).T
    at = slots
    dst_all = everyone[:, at : at + events]
    at += events
    src_all = everyone[:, at : at + events]
    at += events
    gap_all = everyone[:, at : at + events]
    at += events
    count_all = everyone[:, at]

    def reordered(slot):
        place = slot % capacity
        mine = (place // part) == core
        return (slot // capacity) * part + place % part + jnp.where(mine, 0, half)

    dst_all = reordered(dst_all)
    touched_t = touched.T
    me_s = me.reshape(1).astype(jnp.int32)
    freq = jnp.pad(time_freq, (0, CODE - TD)).reshape(1, CODE)
    phase = jnp.pad(time_phase, (0, CODE - TD)).reshape(1, CODE)
    w_msg = jnp.pad(w_msg, ((0, CODE - TD), (0, 0)))
    w_nbr = jnp.pad(w_nbr, ((0, CODE - TD), (0, 0)))

    def call(kernel, name, outs, ins, operands, **more):
        return pl.pallas_call(
            kernel,
            out_shape=outs,
            in_specs=ins,
            compiler_params=params(),
            cost_estimate=cost(10**9, 2**22),
            name=name,
            **more,
        )(*operands)

    table, table_low = call(
        table_kernel,
        "table",
        (shape((GAPS, CODE), BF16),) * 2,
        [VMEM] * 2,
        (freq, phase),
        out_specs=(VMEM,) * 2,
    )
    served, memory_now = pl.pallas_call(
        first_serve_kernel,
        out_shape=(shape((half, DM), BF16), shape((rows, DM), BF16)),
        in_specs=[VMEM] * 2 + [ANY] * 4,
        out_specs=(VMEM,) * 2,
        compiler_params=params(),
        name="first_serve",
    )(serve_t, memory, touched, touched_t, table, w_msg)

    links, code, inv = call(
        links_kernel,
        "links",
        (
            in_hbm((sections, touch, slots), BF16),
            in_hbm((sections, touch, DM), BF16),
            in_hbm((sections, touch, 128), F32),
        ),
        [VMEM] * 3 + [SMEM] + [VMEM] * 2,
        (src_all, dst_all, gap_all, count_all, table, w_msg),
        out_specs=(
            pl.BlockSpec((1, touch, slots), lambda t: (t, 0, 0)),
            pl.BlockSpec((1, touch, DM), lambda t: (t, 0, 0)),
            pl.BlockSpec((1, touch, 128), lambda t: (t, 0, 0)),
        ),
        grid=(sections,),
    )
    lists_t = jnp.concatenate(
        [reordered(nbr_slot[0, 0]), nbr_gap[0, 0], src_slot.reshape(1, events)], axis=0
    ).T
    fresh = memory_now
    snap, keeps = (), ()
    swap = [(i, i ^ 1) for i in range(sections)]
    for turn in range(sections):
        last = turn + 1 == sections
        own = lax.all_to_all(
            served.reshape(shards, part, DM), "node", split_axis=0, concat_axis=0, tiled=True
        ).reshape(half, DM)
        if turn == 1:
            nbr_counts = call(
                neighbours_kernel,
                "neighbour_counts",
                in_hbm((events, slots), BF16),
                [HBM, VMEM],
                (*stay([fresh]), lists_t),
                out_specs=VMEM,
            )
            nbr_codes = call(
                codes_kernel,
                "codes",
                in_hbm((events, CODE), BF16),
                [HBM] + [VMEM] * 3,
                (*stay([fresh]), lists_t, table, table_low),
                out_specs=VMEM,
            )
        if turn < 2:
            beside = stay([links] if turn == 0 else [nbr_counts, nbr_codes, w_nbr])
            own = pl.pallas_call(
                tie_kernel,
                out_shape=shape(own.shape, own.dtype),
                in_specs=[ANY] + [HBM] * len(beside),
                out_specs=ANY,
                input_output_aliases={0: 0},
                compiler_params=params(1),
                name="tie",
            )(own, *beside)
        other = lax.ppermute(own, "tm", swap)
        *ready, memory_now = call(
            functools.partial(ready_kernel, turn, last),
            "ready",
            (
                shape((touch, DM), F32),
                shape((touch, 128), F32),
                shape((touch, half), BF16),
                shape((touch, DM), F32),
                shape((touch, 3 * DM), F32),
                shape((touch, DM), BF16),
                shape((half, DM), BF16),
                shape((half, touch), BF16),
                (in_hbm if turn == 0 else shape)((rows, DM), BF16),
            )
            + (in_hbm((rows, DM), F32),) * (turn > 0),
            [SMEM] + [VMEM] * 8 + [HBM] * (3 + len(snap)),
            (
                me_s,
                own,
                memory_now,
                fresh,
                touched,
                touched_t,
                serve_t,
                w_msg,
                w_hid,
                *stay((links, code, inv) + snap),
            ),
            out_specs=(VMEM,) * 9 + (HBM,) * (turn > 0),
            scratch_shapes=[
                pltpu.VMEM((touch, half), BF16),
                pltpu.VMEM((touch, DM), BF16),
                pltpu.VMEM((rows, DM), F32),
                pltpu.SemaphoreType.DMA((4,)),
                pltpu.SemaphoreType.DMA,
            ],
            input_output_aliases={12: 9} if snap else {},
        )
        if turn > 0:
            snap, memory_now = (memory_now,), ready.pop()
        else:
            snap = ()
        if last:
            break
        fresh, served, *keeps = call(
            functools.partial(update_kernel, turn),
            "update",
            (
                (in_hbm if turn == 0 else shape)((touch, DM), BF16),
                shape((half, DM), BF16),
                in_hbm((slots, DM), BF16),
                in_hbm((touch, DM), BF16),
            ),
            [SMEM] + [VMEM] * 12 + [HBM] * len(keeps),
            (me_s, own, other, *ready, w_msg, w_in, *stay(keeps)),
            out_specs=(VMEM,) * 2 + (HBM,) * 2,
            scratch_shapes=[pltpu.SemaphoreType.DMA((3,))],
            input_output_aliases={13: 2, 14: 3} if keeps else {},
        )
    late = (nbr_counts, nbr_codes, lists_t, w_nbr, w_out)
    emb, snap = call(
        functools.partial(last_kernel, turn),
        "last",
        (in_hbm((events, DM), BF16), in_hbm((rows, DM), F32)),
        [SMEM] * 2 + [VMEM] * 17 + [HBM] * 3,
        (
            me_s,
            count_all,
            own,
            other,
            *ready[:6],
            memory_now,
            w_msg,
            w_in,
            touched,
            *late,
            *stay((*keeps, *snap)),
        ),
        out_specs=(HBM,) * 2,
        scratch_shapes=[
            pltpu.VMEM((slots, DM), BF16),
            pltpu.VMEM((touch, DM), BF16),
            pltpu.VMEM((rows, DM), F32),
            pltpu.VMEM((events, DM), BF16),
            pltpu.SemaphoreType.DMA((2,)),
            pltpu.SemaphoreType.DMA((2,)),
        ],
        input_output_aliases={21: 1},
    )
    return (emb[None, None], snap[None])


def solution(mesh):
    return jax.shard_map(
        body,
        mesh=mesh,
        in_specs=(
            P("node", None),
            P(None, "node", None),
            P("tm", "node", None),
            P("tm", "node"),
            P("tm", "node", None),
            P("tm", "node", None),
            P("tm", "node", None, None),
            P("tm", "node", None),
            P("tm", "node", None, None),
            P(),
            P(),
            P(),
            P(),
            P(),
            P(),
            P(),
        ),
        out_specs=(P("tm", "node", None, None), P("tm", "node", None)),
        check_vma=False,
    )
```

profile of v0, /device:TPU:1, one launch (start us, length us, event | category | flops | bytes accessed | tf_op | source)
XLA Modules:
  0.0 193.3 jit_solution(4734339512658097323)
XLA Ops:
  2.8 6.5 %all-to-all-start = ((s32[8,24,128]{2,1,0:T(8,128)}), s32[8,24,128]{2,1,0:T(8,128)S(1)}, u32[]{:S(2)}, u32[]{:S(2)}) async-start(s32[8,24,128]{2,1,0:T(8,128)} %pack.1), calls=%async_computation | async-start | bytes 196608 | tf_op jit(solution)/shard_map/all_to_all | solution.py:467
  12.5 1.8 table.1
  16.1 10.5 %all-to-all-start.1 = ((bf16[32,16,256]{2,1,0:T(8,128)(2,1)}), bf16[32,16,256]{2,1,0:T(8,128)(2,1)S(1)}, u32[]{:S(2)}, u32[]{:S(2)}) async-start(bf16[32,16,256]{2,1,0:T(8,128)(2,1)} %bitcast.10), calls=%async_computation.1 | async-start | bytes 524288 | tf_op jit(solution)/shard_map/all_to_all | solution.py:548
  26.8 9.9 %links.1 = (bf16[8,256,1024]{2,1,0:T(8,128)(2,1)}, bf16[8,256,256]{2,1,0:T(8,128)(2,1)}, f32[8,256,128]{2,1,0:T(8,128)}) custom-call(s32[8,512]{1,0:T(8,128)S(1)} %get-tuple-element.232.src_ref, s32[8,512]{1,0:T(8,128)S(1)} %get-tuple-element.231.dst_ref, s32[8,512]{1,0:T(8,128)S(1)} %get-tuple-element.230.gap_ref, ...), custom_call_target="tpu_custom_call" | custom-call | flops 1000000000 | bytes 4194304 | tf_op jit(solution)/shard_map/links/pallas_call | solution.py:496
  37.8 2.4 %collective-permute-start = (bf16[512,256]{1,0:T(8,128)(2,1)S(1)}, bf16[512,256]{1,0:T(8,128)(2,1)S(1)}, u32[]{:S(2)}, u32[]{:S(2)}) collective-permute-start(bf16[512,256]{1,0:T(8,128)(2,1)S(1)} %tie.2.own_ref), channel_id=1, source_target_pairs={{0,32},{32,0},{64,96},{96,64},{128,160},{160,128},{192,224},{224,1... | collective-permute-start | bytes 786440 | tf_op jit(solution)/shard_map/ppermute | solution.py:579
  41.0 2.9 %ready.8 = (f32[256,256]{1,0:T(8,128)S(1)}, f32[256,128]{1,0:T(8,128)S(1)}, bf16[256,512]{1,0:T(8,128)(2,1)S(1)}, f32[256,256]{1,0:T(8,128)S(1)}, f32[256,768]{1...) custom-call(s32[1]{0:T(128)} %bitcast.me_ref, ...), custom_call_target="tpu_custom_call" | custom-call | flops 1000000000 | bytes 4194304 | tf_op jit(solution)/shard_map/ready/pallas_call | solution.py:496
  43.9 1.6 update.7
  45.5 7.1 %all-to-all-start.2 = ((bf16[32,16,256]{2,1,0:T(8,128)(2,1)}), bf16[32,16,256]{2,1,0:T(8,128)(2,1)S(1)}, u32[]{:S(2)}, u32[]{:S(2)}) async-start(bf16[32,16,256]{2,1,0:T(8,128)(2,1)} %bitcast.13), calls=%async_computation.2 | async-start | bytes 524288 | tf_op jit(solution)/shard_map/all_to_all | solution.py:548
  52.9 2.6 %neighbour_counts.1.refs_1_.nbr_ref = bf16[512,1024]{1,0:T(8,128)(2,1)} custom-call(bf16[256,256]{1,0:T(8,128)(2,1)} %get-tuple-element.131.after_ref.fresh_ref, s32[512,21]{1,0:T(8,128)S(1)} %bitcast.99), custom_call_target="tpu_custom_call" | custom-call | flops 1000000000 | bytes 4194304 | tf_op jit(solution)/shard_map/neighbour_counts/pallas_call | solution.py:496
  55.5 2.8 %codes.1.refs_2_.codes_ref = bf16[512,128]{1,0:T(8,128)(2,1)} custom-call(bf16[256,256]{1,0:T(8,128)(2,1)} %get-tuple-element.131.after_ref.fresh_ref, s32[512,21]{1,0:T(8,128)S(1)} %bitcast.100, bf16[1024,128]{1,0:T(8,128)(2,1)S(1)} %get-tuple-element.116.rest_2_.table_ref.high_ref, bf16[1024,128]{1,0:T(8,128)(2,1)S(1)} %get-tuple-element.132.low_ref), custom_call_target="tpu_custom_call" | custom-call | flops 1000000000 | bytes 4194304 | tf_op jit(solution)/shard_map/codes/pallas_call | solution.py:496
  58.2 5.8 %all-to-all-done.2 = bf16[32,16,256]{2,1,0:T(8,128)(2,1)S(1)} async-done(((bf16[32,16,256]{2,1,0:T(8,128)(2,1)}), bf16[32,16,256]{2,1,0:T(8,128)(2,1)S(1)}, u32[]{:S(2)}, u32[]{:S(2)}) %all-to-all-start.2) | async-done | bytes 262176 | tf_op jit(solution)/shard_map/all_to_all | solution.py:548
  64.1 2.2 %collective-permute-start.1 = (bf16[512,256]{1,0:T(8,128)(2,1)S(1)}, bf16[512,256]{1,0:T(8,128)(2,1)S(1)}, u32[]{:S(2)}, u32[]{:S(2)}) collective-permute-start(bf16[512,256]{1,0:T(8,128)(2,1)S(1)} %tie.3.own_ref), channel_id=1, source_target_pairs={{0,32},{32,0},{64,96},{96,64},{128,160},{160,128},{192,224},{224,1... | collective-permute-start | bytes 786440 | tf_op jit(solution)/shard_map/ppermute | solution.py:579
  66.3 1.8 ready.9
  68.1 1.5 update.8
  69.6 16.6 %all_to_all.45 = bf16[32,16,256]{2,1,0:T(8,128)(2,1)S(1)} all-to-all(bf16[32,16,256]{2,1,0:T(8,128)(2,1)S(1)} %bitcast.112), channel_id=1, replica_groups=mesh['tm'=8,'node'=32] {'node'}, dimensions={0} | all-to-all | bytes 524288 | tf_op jit(solution)/shard_map/all_to_all | solution.py:548
  86.5 2.0 %ready.10 = (f32[256,256]{1,0:T(8,128)S(1)}, f32[256,128]{1,0:T(8,128)S(1)}, bf16[256,512]{1,0:T(8,128)(2,1)S(1)}, f32[256,256]{1,0:T(8,128)S(1)}, f32[256,768]{...) custom-call(s32[1]{0:T(128)} %bitcast.me_ref, ...), custom_call_target="tpu_custom_call", output_to_operand_aliasing={{9}: (12, {})} | custom-call | flops 1000000000 | bytes 4194304 | tf_op jit(solution)/shard_map/ready/pallas_call | solution.py:496
  89.4 16.0 %all_to_all.46 = bf16[32,16,256]{2,1,0:T(8,128)(2,1)S(1)} all-to-all(bf16[32,16,256]{2,1,0:T(8,128)(2,1)S(1)} %bitcast.113), channel_id=1, replica_groups=mesh['tm'=8,'node'=32] {'node'}, dimensions={0} | all-to-all | bytes 524288 | tf_op jit(solution)/shard_map/all_to_all | solution.py:548
  105.4 1.9 collective-permute-start.3
  107.3 1.8 ready.11
  110.0 15.3 %all_to_all.47 = bf16[32,16,256]{2,1,0:T(8,128)(2,1)S(1)} all-to-all(bf16[32,16,256]{2,1,0:T(8,128)(2,1)S(1)} %bitcast.114), channel_id=1, replica_groups=mesh['tm'=8,'node'=32] {'node'}, dimensions={0} | all-to-all | bytes 524288 | tf_op jit(solution)/shard_map/all_to_all | solution.py:548
  125.3 1.9 collective-permute-start.4
  127.2 1.8 ready.12
  129.9 15.3 %all_to_all.48 = bf16[32,16,256]{2,1,0:T(8,128)(2,1)S(1)} all-to-all(bf16[32,16,256]{2,1,0:T(8,128)(2,1)S(1)} %bitcast.115), channel_id=1, replica_groups=mesh['tm'=8,'node'=32] {'node'}, dimensions={0} | all-to-all | bytes 524288 | tf_op jit(solution)/shard_map/all_to_all | solution.py:548
  145.2 2.0 %collective-permute-start.5 = (bf16[512,256]{1,0:T(8,128)(2,1)S(1)}, bf16[512,256]{1,0:T(8,128)(2,1)S(1)}, u32[]{:S(2)}, u32[]{:S(2)}) collective-permute-start(bf16[512,256]{1,0:T(8,128)(2,1)S(1)} %bitcast.89), channel_id=1, source_target_pairs={{0,32},{32,0},{64,96},{96,64},{128,160},{160,128},{192,224},{224,1... | collective-permute-start | bytes 786440 | tf_op jit(solution)/shard_map/ppermute | solution.py:579
  147.1 1.8 ready.13
  149.8 15.3 %all_to_all.49 = bf16[32,16,256]{2,1,0:T(8,128)(2,1)S(1)} all-to-all(bf16[32,16,256]{2,1,0:T(8,128)(2,1)S(1)} %bitcast.116), channel_id=1, replica_groups=mesh['tm'=8,'node'=32] {'node'}, dimensions={0} | all-to-all | bytes 524288 | tf_op jit(solution)/shard_map/all_to_all | solution.py:548
  165.1 2.0 %collective-permute-start.6 = (bf16[512,256]{1,0:T(8,128)(2,1)S(1)}, bf16[512,256]{1,0:T(8,128)(2,1)S(1)}, u32[]{:S(2)}, u32[]{:S(2)}) collective-permute-start(bf16[512,256]{1,0:T(8,128)(2,1)S(1)} %bitcast.92), channel_id=1, source_target_pairs={{0,32},{32,0},{64,96},{96,64},{128,160},{160,128},{192,224},{224,1... | collective-permute-start | bytes 786440 | tf_op jit(solution)/shard_map/ppermute | solution.py:579
  167.1 1.8 ready.14
  169.7 15.3 %all_to_all.50 = bf16[32,16,256]{2,1,0:T(8,128)(2,1)S(1)} all-to-all(bf16[32,16,256]{2,1,0:T(8,128)(2,1)S(1)} %bitcast.117), channel_id=1, replica_groups=mesh['tm'=8,'node'=32] {'node'}, dimensions={0} | all-to-all | bytes 524288 | tf_op jit(solution)/shard_map/all_to_all | solution.py:548
  185.0 2.0 %collective-permute-start.7 = (bf16[512,256]{1,0:T(8,128)(2,1)S(1)}, bf16[512,256]{1,0:T(8,128)(2,1)S(1)}, u32[]{:S(2)}, u32[]{:S(2)}) collective-permute-start(bf16[512,256]{1,0:T(8,128)(2,1)S(1)} %bitcast.96), channel_id=1, source_target_pairs={{0,32},{32,0},{64,96},{96,64},{128,160},{160,128},{192,224},{224,1... | collective-permute-start | bytes 786440 | tf_op jit(solution)/shard_map/ppermute | solution.py:579
  187.0 2.5 %ready.15 = (f32[256,256]{1,0:T(8,128)S(1)}, f32[256,128]{1,0:T(8,128)S(1)}, bf16[256,512]{1,0:T(8,128)(2,1)S(1)}, f32[256,256]{1,0:T(8,128)S(1)}, f32[256,768]{...) custom-call(s32[1]{0:T(128)} %bitcast.me_ref, ...), custom_call_target="tpu_custom_call", output_to_operand_aliasing={{9}: (12, {})} | custom-call | flops 1000000000 | bytes 4194304 | tf_op jit(solution)/shard_map/ready/pallas_call | solution.py:496
  189.5 3.6 %last.1 = (bf16[512,256]{1,0:T(8,128)(2,1)}, f32[512,256]{1,0:T(8,128)}) custom-call(s32[1]{0:T(128)} %bitcast.me_ref, s32[8]{0:T(128)S(1)} %slice_reduce_fusion.count_ref.counts_ref, bf16[512,256]{1,0:T(8,128)(2,1)S(1)} %bitcast.98, bf16[512,256]{1,0:T(8,128)(2,1)S(1)} %collective-permute-done.7.other_ref, ...), custom_call_target="tpu_custom_call", output_to_operand_aliasing={{1}: (21, {})} | custom-call | flops 1000000000 | bytes 4194304 | tf_op jit(solution)/shard_map/last/pallas_call | solution.py:496
  (62 shorter events, 13.4 us)
Async XLA Ops:
  0.6 14.4 %copy-start.4 = (f32[512,256]{1,0:T(8,128)S(1)}, f32[512,256]{1,0:T(8,128)}, u32[]{:S(2)}) copy-start(f32[512,256]{1,0:T(8,128)} %memory_ref.1) | copy-start | bytes 1572868
  2.8 11.5 %all-to-all-start = ((s32[8,24,128]{2,1,0:T(8,128)}), s32[8,24,128]{2,1,0:T(8,128)S(1)}, u32[]{:S(2)}, u32[]{:S(2)}) async-start(s32[8,24,128]{2,1,0:T(8,128)} %pack.1), calls=%async_computation | async-start | bytes 196608 | tf_op jit(solution)/shard_map/all_to_all | solution.py:467
  16.1 21.7 %all-to-all-start.1 = ((bf16[32,16,256]{2,1,0:T(8,128)(2,1)}), bf16[32,16,256]{2,1,0:T(8,128)(2,1)S(1)}, u32[]{:S(2)}, u32[]{:S(2)}) async-start(bf16[32,16,256]{2,1,0:T(8,128)(2,1)} %bitcast.10), calls=%async_computation.1 | async-start | bytes 524288 | tf_op jit(solution)/shard_map/all_to_all | solution.py:548
  26.8 13.5 %copy-start.10 = (s32[1,1,10,512]{3,1,2,0:T(1,128)S(1)}, s32[1,1,10,512]{3,1,2,0:T(1,128)}, u32[]{:S(2)}) copy-start(s32[1,1,10,512]{3,1,2,0:T(1,128)} %param.24) | copy-start | bytes 61444
  26.8 13.5 %copy-start.9 = (bf16[356,256]{1,0:T(8,128)(2,1)S(1)}, bf16[356,256]{1,0:T(8,128)(2,1)}, u32[]{:S(2)}) copy-start(bf16[356,256]{1,0:T(8,128)(2,1)} %param.30) | copy-start | bytes 546820
  26.8 14.2 %copy-start = (bf16[256,768]{1,0:T(8,128)(2,1)S(1)}, bf16[256,768]{1,0:T(8,128)(2,1)}, u32[]{:S(2)}) copy-start(bf16[256,768]{1,0:T(8,128)(2,1)} %w_hid_ref.15) | copy-start | bytes 1179652
  37.8 6.0 %collective-permute-start = (bf16[512,256]{1,0:T(8,128)(2,1)S(1)}, bf16[512,256]{1,0:T(8,128)(2,1)S(1)}, u32[]{:S(2)}, u32[]{:S(2)}) collective-permute-start(bf16[512,256]{1,0:T(8,128)(2,1)S(1)} %tie.2.own_ref), channel_id=1, source_target_pairs={{0,32},{32,0},{64,96},{96,64},{128,160},{160,128},{192,224},{224,1... | collective-permute-start | bytes 786440 | tf_op jit(solution)/shard_map/ppermute | solution.py:579
  41.0 2.9 %copy-start.1 = (bf16[256,768]{1,0:T(8,128)(2,1)S(1)}, bf16[256,768]{1,0:T(8,128)(2,1)}, u32[]{:S(2)}) copy-start(bf16[256,768]{1,0:T(8,128)(2,1)} %w_in_ref.15) | copy-start | bytes 1179652
  41.0 11.6 %copy-start.11 = (s32[1,1,10,512]{3,1,2,0:T(1,128)S(1)}, s32[1,1,10,512]{3,1,2,0:T(1,128)}, u32[]{:S(2)}) copy-start(s32[1,1,10,512]{3,1,2,0:T(1,128)} %param.22) | copy-start | bytes 61444
  43.9 8.8 %copy-start.12 = (s32[1,1,512]{2,1,0:T(1,128)S(1)}, s32[1,1,512]{2,1,0:T(1,128)}, u32[]{:S(2)}) copy-start(s32[1,1,512]{2,1,0:T(1,128)} %param.18) | copy-start | bytes 6148
  45.5 18.5 %all-to-all-start.2 = ((bf16[32,16,256]{2,1,0:T(8,128)(2,1)}), bf16[32,16,256]{2,1,0:T(8,128)(2,1)S(1)}, u32[]{:S(2)}, u32[]{:S(2)}) async-start(bf16[32,16,256]{2,1,0:T(8,128)(2,1)} %bitcast.13), calls=%async_computation.2 | async-start | bytes 524288 | tf_op jit(solution)/shard_map/all_to_all | solution.py:548
  52.9 13.4 %copy-start.6 = (bf16[512,256]{1,0:T(8,128)(2,1)S(1)}, bf16[512,256]{1,0:T(8,128)(2,1)}, u32[]{:S(2)}) copy-start(bf16[512,256]{1,0:T(8,128)(2,1)} %get-tuple-element.133.kept_ref) | copy-start | bytes 786436
  52.9 13.4 %copy-start.8 = (bf16[256,256]{1,0:T(8,128)(2,1)S(1)}, bf16[256,256]{1,0:T(8,128)(2,1)}, u32[]{:S(2)}) copy-start(bf16[256,256]{1,0:T(8,128)(2,1)} %get-tuple-element.131.after_ref.fresh_ref) | copy-start | bytes 393220
  64.1 4.0 %collective-permute-start.1 = (bf16[512,256]{1,0:T(8,128)(2,1)S(1)}, bf16[512,256]{1,0:T(8,128)(2,1)S(1)}, u32[]{:S(2)}, u32[]{:S(2)}) collective-permute-start(bf16[512,256]{1,0:T(8,128)(2,1)S(1)} %tie.3.own_ref), channel_id=1, source_target_pairs={{0,32},{32,0},{64,96},{96,64},{128,160},{160,128},{192,224},{224,1... | collective-permute-start | bytes 786440 | tf_op jit(solution)/shard_map/ppermute | solution.py:579
  86.1 2.4 %collective-permute-start.2 = (bf16[512,256]{1,0:T(8,128)(2,1)S(1)}, bf16[512,256]{1,0:T(8,128)(2,1)S(1)}, u32[]{:S(2)}, u32[]{:S(2)}) collective-permute-start(bf16[512,256]{1,0:T(8,128)(2,1)S(1)} %bitcast.80), channel_id=1, source_target_pairs={{0,32},{32,0},{64,96},{96,64},{128,160},{160,128},{192,224},{224,1... | collective-permute-start | bytes 786440 | tf_op jit(solution)/shard_map/ppermute | solution.py:579
  105.4 3.6 %collective-permute-start.3 = (bf16[512,256]{1,0:T(8,128)(2,1)S(1)}, bf16[512,256]{1,0:T(8,128)(2,1)S(1)}, u32[]{:S(2)}, u32[]{:S(2)}) collective-permute-start(bf16[512,256]{1,0:T(8,128)(2,1)S(1)} %bitcast.83), channel_id=1, source_target_pairs={{0,32},{32,0},{64,96},{96,64},{128,160},{160,128},{192,224},{224,1... | collective-permute-start | bytes 786440 | tf_op jit(solution)/shard_map/ppermute | solution.py:579
  125.3 3.7 %collective-permute-start.4 = (bf16[512,256]{1,0:T(8,128)(2,1)S(1)}, bf16[512,256]{1,0:T(8,128)(2,1)S(1)}, u32[]{:S(2)}, u32[]{:S(2)}) collective-permute-start(bf16[512,256]{1,0:T(8,128)(2,1)S(1)} %bitcast.86), channel_id=1, source_target_pairs={{0,32},{32,0},{64,96},{96,64},{128,160},{160,128},{192,224},{224,1... | collective-permute-start | bytes 786440 | tf_op jit(solution)/shard_map/ppermute | solution.py:579
  145.2 3.8 %collective-permute-start.5 = (bf16[512,256]{1,0:T(8,128)(2,1)S(1)}, bf16[512,256]{1,0:T(8,128)(2,1)S(1)}, u32[]{:S(2)}, u32[]{:S(2)}) collective-permute-start(bf16[512,256]{1,0:T(8,128)(2,1)S(1)} %bitcast.89), channel_id=1, source_target_pairs={{0,32},{32,0},{64,96},{96,64},{128,160},{160,128},{192,224},{224,1... | collective-permute-start | bytes 786440 | tf_op jit(solution)/shard_map/ppermute | solution.py:579
  165.1 3.8 %collective-permute-start.6 = (bf16[512,256]{1,0:T(8,128)(2,1)S(1)}, bf16[512,256]{1,0:T(8,128)(2,1)S(1)}, u32[]{:S(2)}, u32[]{:S(2)}) collective-permute-start(bf16[512,256]{1,0:T(8,128)(2,1)S(1)} %bitcast.92), channel_id=1, source_target_pairs={{0,32},{32,0},{64,96},{96,64},{128,160},{160,128},{192,224},{224,1... | collective-permute-start | bytes 786440 | tf_op jit(solution)/shard_map/ppermute | solution.py:579
  185.0 4.5 %collective-permute-start.7 = (bf16[512,256]{1,0:T(8,128)(2,1)S(1)}, bf16[512,256]{1,0:T(8,128)(2,1)S(1)}, u32[]{:S(2)}, u32[]{:S(2)}) collective-permute-start(bf16[512,256]{1,0:T(8,128)(2,1)S(1)} %bitcast.96), channel_id=1, source_target_pairs={{0,32},{32,0},{64,96},{96,64},{128,160},{160,128},{192,224},{224,1... | collective-permute-start | bytes 786440 | tf_op jit(solution)/shard_map/ppermute | solution.py:579
  187.0 2.5 %copy-start.2 = (bf16[512,1024]{1,0:T(8,128)(2,1)S(1)}, bf16[512,1024]{1,0:T(8,128)(2,1)}, u32[]{:S(2)}) copy-start(bf16[512,1024]{1,0:T(8,128)(2,1)} %neighbour_counts.1.refs_1_.nbr_ref) | copy-start | bytes 3145732
  187.0 2.5 %copy-start.3 = (bf16[384,256]{1,0:T(8,128)(2,1)S(1)}, bf16[384,256]{1,0:T(8,128)(2,1)}, u32[]{:S(2)}) copy-start(bf16[384,256]{1,0:T(8,128)(2,1)} %pad.18.refs_3_.w_nbr_ref) | copy-start | bytes 589828
  187.0 2.5 %copy-start.5 = (bf16[512,128]{1,0:T(8,128)(2,1)S(1)}, bf16[512,128]{1,0:T(8,128)(2,1)}, u32[]{:S(2)}) copy-start(bf16[512,128]{1,0:T(8,128)(2,1)} %codes.1.refs_2_.codes_ref) | copy-start | bytes 393220
  187.0 2.5 %copy-start.7 = (bf16[512,256]{1,0:T(8,128)(2,1)S(1)}, bf16[512,256]{1,0:T(8,128)(2,1)}, u32[]{:S(2)}) copy-start(bf16[512,256]{1,0:T(8,128)(2,1)} %w_out_ref.1) | copy-start | bytes 786436
where the time goes:
time: 194 us; the launch traced here: 193 us
  blocking collectives  93.7 us (48%)
  Pallas kernels  46.8 us (24%)
  starting transfers between devices  38.9 us (20%)
  waiting for transfers between devices  6.9 us (4%)
  local copies, waits for them, and re-layouts  4.76 us (2%)
  between operations  1.96 us (1%)
    all_to_all x6, blocking collectives, body(): lax.all_to_all(served.reshape(shards, part, DM), 'node', split_axis=0, co...  93.7 us
    pallas_call x20, Pallas kernels, call(): pl.pallas_call(kernel, out_shape=outs, in_specs=ins, compiler_params=para...  44.3 us
    all_to_all x2, starting transfers between devices, body(): lax.all_to_all(served.reshape(shards, part, DM), 'node', split_axis=0, co...  17.6 us
    ppermute x8, starting transfers between devices, body(): other = lax.ppermute(own, 'tm', swap)  14.8 us
    all_to_all x2, waiting for transfers between devices, body(): lax.all_to_all(served.reshape(shards, part, DM), 'node', split_axis=0, co...  6.87 us
    all_to_all x1, starting transfers between devices, body(): lax.all_to_all(packed, 'tm', split_axis=0, concat_axis=0, tiled=True)  6.52 us
  transfers between devices with their start and end apart: 11, of which 2 were waited for; matrix products, arithmetic and copies ran while one was open for 2% of the time, Pallas kernels for 17%

commit v1 on v0

--- a/solution.py
+++ b/solution.py
@@ -12,6 +12,7 @@
 CODE = 128
 GAPS = 1024
 NBRS = 10
+FIRST = 5
 F32 = jnp.float32
 BF16 = jnp.bfloat16
 VMEM = pl.BlockSpec(memory_space=pltpu.VMEM)
@@ -32,10 +33,6 @@
     return lax.broadcasted_iota(jnp.int32, shape, axis)
 
 
-def ones_where(mask):
-    return jnp.where(mask, 1.0, 0.0).astype(BF16)
-
-
 def same16(a, b):
     mask = a.astype(jnp.int16) == b.astype(jnp.int16)
     return jnp.where(mask, jnp.ones((), BF16), jnp.zeros((), BF16))
@@ -53,10 +50,6 @@
 def split_two(x):
     high = x.astype(BF16)
     return high, (x - high.astype(F32)).astype(BF16)
-
-
-def hit_rows(place):
-    return jnp.max(place.astype(F32), axis=1, keepdims=True) > 0.5
 
 
 def copies(pairs, sems):
@@ -96,8 +89,8 @@
     low_out[...] = low
 
 
-def links_kernel(src_ref, dst_ref, gap_ref, count_ref, table_ref, w_code_ref, links_out, code_out, inv_out):
-    turn = pl.program_id(0)
+def links_kernel(begin, after_ref, src_ref, dst_ref, gap_ref, count_ref, table_ref, w_code_ref, links_out, code_out, inv_out):
+    turn = begin + pl.program_id(0)
     touch, slots = links_out.shape[1:]
     events = src_ref.shape[1]
     row = pl.ds(turn, 1)
@@ -117,14 +110,12 @@
 
 def ready_kernel(
     turn,
-    last,
+    at,
     me_ref,
     own_ref,
-    kept_ref,
-    fresh_ref,
+    memory_ref,
     touched_ref,
     touched_t_ref,
-    serve_t_ref,
     w_msg_ref,
     w_hid_ref,
     links_ref,
@@ -132,25 +123,23 @@
     inv_ref,
     *rest,
 ):
-    outs = rest[turn > 1 : (turn > 1) + 9]
-    total_out, inv_out, links_out, base_out, gh_out, held_out, static_out, hits_out, kept_out = outs
+    outs = rest[turn > 1 : (turn > 1) + 7]
+    total_out, inv_out, links_out, base_out, gh_out, held_out, kept_out = outs
     links_scr, code_scr, memory_scr, sems, snap_sem = rest[-5:]
-    rows, touch, half = kept_ref.shape[0], touched_ref.shape[1], own_ref.shape[0]
+    rows, touch, half = memory_ref.shape[0], touched_ref.shape[1], own_ref.shape[0]
     loads = copies(
         [
-            (links_ref.at[turn, :, :half], links_scr),
-            (links_ref.at[turn, :, half:], links_out),
-            (code_ref.at[turn], code_scr),
-            (inv_ref.at[turn], inv_out),
+            (links_ref.at[at, :, :half], links_scr),
+            (links_ref.at[at, :, half:], links_out),
+            (code_ref.at[at], code_scr),
+            (inv_ref.at[at], inv_out),
         ],
         sems,
     )
     for copy in loads:
         copy.start()
-    memory = kept_ref[...]
+    memory = memory_ref[...]
     if turn > 0:
-        place = pick_rows(rows, touched_ref[turn - 1 : turn, :])
-        memory = memory + dot(place, fresh_ref[...]).astype(BF16)
         snap_store = pltpu.make_async_copy(memory_scr, rest[-6], snap_sem)
 
         @pl.when(me_ref[0] == turn - 1)
@@ -166,13 +155,7 @@
     now = touched_ref[turn : turn + 1, :]
     hit = dot(pick_rows(rows, now), jnp.ones((touch, 128), BF16))
     free = (1.0 - hit).astype(BF16)
-    kept = memory * jnp.concatenate([free, free], axis=1)
-    kept_out[...] = kept
-    if not last:
-        wanted = serve_t_ref[:, turn + 1 : turn + 2]
-        serve = same16(wanted, iota((half, rows), 1))
-        static_out[...] = dot(serve, kept).astype(BF16)
-        hits_out[...] = same16(wanted, now)
+    kept_out[...] = memory * jnp.concatenate([free, free], axis=1)
     loads[0].wait()
     total_out[...] = dot(links_scr[...], own_ref[...])
     loads[2].wait()
@@ -208,20 +191,21 @@
     base_ref,
     gh_ref,
     held_ref,
-    static_ref,
-    hits_ref,
+    memory_ref,
+    touched_ref,
+    serve_t_ref,
     w_msg_ref,
     w_in_ref,
     *rest,
 ):
-    fresh_out, served_out, kept_out, fresh_kept_out, kept_sems = rest[-5:]
-    half = own_ref.shape[0]
+    memory_out, served_out, kept_out, fresh_kept_out, fresh_scr, kept_sems = rest[-6:]
+    half, rows = own_ref.shape[0], memory_ref.shape[0]
     mine = me_ref[0] == turn
     keeps = copies(
         [
             (own_ref, kept_out.at[:half]),
             (other_ref, kept_out.at[half:]),
-            (fresh_out, fresh_kept_out),
+            (fresh_scr, fresh_kept_out),
         ],
         kept_sems,
     )
@@ -241,33 +225,19 @@
         held_ref[...],
         w_msg_ref[DM : 2 * DM, :],
         w_in_ref[...],
-    )
-    fresh_b = fresh.astype(BF16)
-    fresh_out[...] = fresh_b
+    ).astype(BF16)
+    place = pick_rows(rows, touched_ref[turn : turn + 1, :])
+    memory = memory_ref[...] + dot(place, fresh).astype(BF16)
+    serve = same16(serve_t_ref[:, turn + 1 : turn + 2], iota((half, rows), 1))
+    served_out[...] = dot(serve, memory).astype(BF16)
+    memory_out[...] = memory
 
     @pl.when(mine)
     def _():
+        fresh_scr[...] = fresh
         keeps[2].start()
-
-    served = dot(hits_ref[...], fresh_b) + static_ref[...].astype(F32)
-    served_out[...] = served.astype(BF16)
-
-    @pl.when(mine)
-    def _():
         for copy in keeps:
             copy.wait()
-
-
-def embedded(live_count, nbr, kept, codes, src_t, fresh_b, w_nbr, w_nbr_code, w_out):
-    events = src_t.shape[0]
-    near = dot(nbr, kept)
-    hidden = dot(near.astype(BF16), w_nbr) + dot(codes, w_nbr_code)
-    hidden = jnp.maximum(hidden, 0.0).astype(BF16)
-    src_pick = same16(src_t, iota((events, fresh_b.shape[0]), 1))
-    src_new = dot(src_pick, fresh_b).astype(BF16)
-    out = dot(src_new, w_out[:DM, :]) + dot(hidden, w_out[DM:, :])
-    live = iota((events, 1), 0) < live_count
-    return jnp.where(live, out, 0.0).astype(BF16)
 
 
 def last_kernel(
@@ -296,66 +266,61 @@
     snap_in_ref,
     emb_out,
     snap_out,
-    rows_scr,
-    fresh_scr,
     snap_scr,
     emb_scr,
-    rows_sems,
-    out_sems,
+    sems,
 ):
     mine = me_ref[0] == turn
     half = own_ref.shape[0]
-    early = copies([(rows_ref, rows_scr), (fresh_kept_ref, fresh_scr)], rows_sems)
-    snap_store = pltpu.make_async_copy(snap_scr, snap_out, out_sems.at[0])
-
-    @pl.when(jnp.logical_not(mine))
-    def _():
-        for copy in early:
-            copy.start()
-        for copy in early:
-            copy.wait()
+    events = emb_scr.shape[0]
+    rows, touch = memory_ref.shape[0], touched_ref.shape[1]
+    snap_store = pltpu.make_async_copy(snap_scr, snap_out, sems.at[0])
+    own = jnp.where(mine, own_ref[...], rows_ref[:half, :])
+    other = jnp.where(mine, other_ref[...], rows_ref[half:, :])
+    near = dot(nbr_ref[:, :half], own) + dot(nbr_ref[:, half:], other)
+    hidden = dot(near.astype(BF16), w_nbr_ref[:DM, :]) + dot(codes_ref[...], w_nbr_ref[DM:, :])
+    hidden = jnp.maximum(hidden, 0.0).astype(BF16)
+    lower = dot(hidden, w_out_ref[DM:, :])
+    fresh = updated(
+        other_ref[...],
+        total_ref[...],
+        inv_ref[...],
+        links_ref[...],
+        base_ref[...],
+        gh_ref[...],
+        held_ref[...],
+        w_msg_ref[DM : 2 * DM, :],
+        w_in_ref[...],
+    )
+    place = pick_rows(rows, touched_ref[turn : turn + 1, :])
+    high, low = split_two(fresh)
+    snap_scr[...] = memory_ref[...].astype(F32) + (dot(place, high) + dot(place, low))
 
     @pl.when(mine)
     def _():
-        rows_scr[:half, :] = own_ref[...]
-        rows_scr[half:, :] = other_ref[...]
-        fresh = updated(
-            other_ref[...],
-            total_ref[...],
-            inv_ref[...],
-            links_ref[...],
-            base_ref[...],
-            gh_ref[...],
-            held_ref[...],
-            w_msg_ref[DM : 2 * DM, :],
-            w_in_ref[...],
-        )
-        fresh_scr[...] = fresh.astype(BF16)
-        rows, touch = memory_ref.shape[0], touched_ref.shape[1]
-        place = pick_rows(rows, touched_ref[turn : turn + 1, :])
-        high, low = split_two(fresh)
-        snap_scr[...] = memory_ref[...].astype(F32) + (dot(place, high) + dot(place, low))
         snap_store.start()
 
-    emb_scr[...] = embedded(
-        counts_ref[me_ref[0]],
-        nbr_ref[...],
-        rows_scr[...],
-        codes_ref[...],
-        lists_ref[:, 2 * NBRS : 2 * NBRS + 1],
-        fresh_scr[...],
-        w_nbr_ref[:DM, :],
-        w_nbr_ref[DM:, :],
-        w_out_ref,
-    )
-    store_emb = pltpu.make_async_copy(emb_scr, emb_out, out_sems.at[1])
-    store_emb.start()
+    fresh = jnp.where(mine, high, fresh_kept_ref[...])
+    block = events // 2
+    stores = []
+    for i in range(2):
+        at = slice(i * block, (i + 1) * block)
+        sources = lists_ref[at, 2 * NBRS : 2 * NBRS + 1]
+        src_pick = same16(sources, iota((block, touch), 1))
+        src_new = dot(src_pick, fresh).astype(BF16)
+        out = dot(src_new, w_out_ref[:DM, :]) + lower[at, :]
+        live = iota((block, 1), 0) + i * block < counts_ref[me_ref[0]]
+        emb_scr[at, :] = jnp.where(live, out, 0.0).astype(BF16)
+        store = pltpu.make_async_copy(emb_scr.at[at], emb_out.at[at], sems.at[1 + i])
+        store.start()
+        stores.append(store)
 
     @pl.when(mine)
     def _():
         snap_store.wait()
 
-    store_emb.wait()
+    for store in stores:
+        store.wait()
 
 
 def count_block(lists, number, begin, width):
@@ -514,37 +479,39 @@
     served, memory_now = pl.pallas_call(
         first_serve_kernel,
         out_shape=(shape((half, DM), BF16), shape((rows, DM), BF16)),
-        in_specs=[VMEM] * 2 + [ANY] * 4,
+        in_specs=[VMEM] * 2 + [ANY] * 2,
         out_specs=(VMEM,) * 2,
         compiler_params=params(),
         name="first_serve",
-    )(serve_t, memory, touched, touched_t, table, w_msg)
-
-    links, code, inv = call(
-        links_kernel,
-        "links",
-        (
-            in_hbm((sections, touch, slots), BF16),
-            in_hbm((sections, touch, DM), BF16),
-            in_hbm((sections, touch, 128), F32),
-        ),
-        [VMEM] * 3 + [SMEM] + [VMEM] * 2,
-        (src_all, dst_all, gap_all, count_all, table, w_msg),
-        out_specs=(
-            pl.BlockSpec((1, touch, slots), lambda t: (t, 0, 0)),
-            pl.BlockSpec((1, touch, DM), lambda t: (t, 0, 0)),
-            pl.BlockSpec((1, touch, 128), lambda t: (t, 0, 0)),
-        ),
-        grid=(sections,),
-    )
+    )(serve_t, memory, touched, touched_t)
+
+    def make_links(begin, number, after):
+        return call(
+            functools.partial(links_kernel, begin),
+            "links",
+            (
+                in_hbm((number, touch, slots), BF16),
+                in_hbm((number, touch, DM), BF16),
+                in_hbm((number, touch, 128), F32),
+            ),
+            [HBM] + [VMEM] * 3 + [SMEM] + [VMEM] * 2,
+            (*stay([after]), src_all, dst_all, gap_all, count_all, table, w_msg),
+            out_specs=(
+                pl.BlockSpec((1, touch, slots), lambda t: (t, 0, 0)),
+                pl.BlockSpec((1, touch, DM), lambda t: (t, 0, 0)),
+                pl.BlockSpec((1, touch, 128), lambda t: (t, 0, 0)),
+            ),
+            grid=(number,),
+        )
+
+    split = min(FIRST, sections)
+    parts = [make_links(0, split, memory)]
     lists_t = jnp.concatenate(
         [reordered(nbr_slot[0, 0]), nbr_gap[0, 0], src_slot.reshape(1, events)], axis=0
     ).T
-    fresh = memory_now
     snap, keeps = (), ()
     swap = [(i, i ^ 1) for i in range(sections)]
     for turn in range(sections):
-        last = turn + 1 == sections
         own = lax.all_to_all(
             served.reshape(shards, part, DM), "node", split_axis=0, concat_axis=0, tiled=True
         ).reshape(half, DM)
@@ -554,7 +521,7 @@
                 "neighbour_counts",
                 in_hbm((events, slots), BF16),
                 [HBM, VMEM],
-                (*stay([fresh]), lists_t),
+                (*stay([memory_now]), lists_t),
                 out_specs=VMEM,
             )
             nbr_codes = call(
@@ -562,11 +529,12 @@
                 "codes",
                 in_hbm((events, CODE), BF16),
                 [HBM] + [VMEM] * 3,
-                (*stay([fresh]), lists_t, table, table_low),
+                (*stay([memory_now]), lists_t, table, table_low),
                 out_specs=VMEM,
             )
+            parts.append(make_links(split, sections - split, memory_now))
         if turn < 2:
-            beside = stay([links] if turn == 0 else [nbr_counts, nbr_codes, w_nbr])
+            beside = stay([parts[0][0]] if turn == 0 else [nbr_counts, nbr_codes, parts[1][0]])
             own = pl.pallas_call(
                 tie_kernel,
                 out_shape=shape(own.shape, own.dtype),
@@ -577,8 +545,9 @@
                 name="tie",
             )(own, *beside)
         other = lax.ppermute(own, "tm", swap)
-        *ready, memory_now = call(
-            functools.partial(ready_kernel, turn, last),
+        late_links = turn >= split
+        outs = call(
+            functools.partial(ready_kernel, turn, turn - split * late_links),
             "ready",
             (
                 shape((touch, DM), F32),
@@ -587,25 +556,21 @@
                 shape((touch, DM), F32),
                 shape((touch, 3 * DM), F32),
                 shape((touch, DM), BF16),
-                shape((half, DM), BF16),
-                shape((half, touch), BF16),
-                (in_hbm if turn == 0 else shape)((rows, DM), BF16),
+                shape((rows, DM), BF16),
             )
             + (in_hbm((rows, DM), F32),) * (turn > 0),
-            [SMEM] + [VMEM] * 8 + [HBM] * (3 + len(snap)),
+            [SMEM] + [VMEM] * 6 + [HBM] * (3 + len(snap)),
             (
                 me_s,
                 own,
                 memory_now,
-                fresh,
                 touched,
                 touched_t,
-                serve_t,
                 w_msg,
                 w_hid,
-                *stay((links, code, inv) + snap),
+                *stay((*parts[late_links], *snap)),
             ),
-            out_specs=(VMEM,) * 9 + (HBM,) * (turn > 0),
+            out_specs=(VMEM,) * 7 + (HBM,) * (turn > 0),
             scratch_shapes=[
                 pltpu.VMEM((touch, half), BF16),
                 pltpu.VMEM((touch, DM), BF16),
@@ -613,56 +578,50 @@
                 pltpu.SemaphoreType.DMA((4,)),
                 pltpu.SemaphoreType.DMA,
             ],
-            input_output_aliases={12: 9} if snap else {},
+            input_output_aliases={10: 7} if snap else {},
         )
-        if turn > 0:
-            snap, memory_now = (memory_now,), ready.pop()
-        else:
-            snap = ()
-        if last:
+        ready, snap = outs[:7], outs[7:]
+        if turn + 1 == sections:
             break
-        fresh, served, *keeps = call(
+        memory_now, served, *keeps = call(
             functools.partial(update_kernel, turn),
             "update",
             (
-                (in_hbm if turn == 0 else shape)((touch, DM), BF16),
+                (in_hbm if turn == 0 else shape)((rows, DM), BF16),
                 shape((half, DM), BF16),
                 in_hbm((slots, DM), BF16),
                 in_hbm((touch, DM), BF16),
             ),
-            [SMEM] + [VMEM] * 12 + [HBM] * len(keeps),
-            (me_s, own, other, *ready, w_msg, w_in, *stay(keeps)),
+            [SMEM] + [VMEM] * 13 + [HBM] * len(keeps),
+            (me_s, own, other, *ready, touched, serve_t, w_msg, w_in, *stay(keeps)),
             out_specs=(VMEM,) * 2 + (HBM,) * 2,
-            scratch_shapes=[pltpu.SemaphoreType.DMA((3,))],
-            input_output_aliases={13: 2, 14: 3} if keeps else {},
+            scratch_shapes=[pltpu.VMEM((touch, DM), BF16), pltpu.SemaphoreType.DMA((3,))],
+            input_output_aliases={14: 2, 15: 3} if keeps else {},
         )
     late = (nbr_counts, nbr_codes, lists_t, w_nbr, w_out)
     emb, snap = call(
         functools.partial(last_kernel, turn),
         "last",
         (in_hbm((events, DM), BF16), in_hbm((rows, DM), F32)),
-        [SMEM] * 2 + [VMEM] * 17 + [HBM] * 3,
+        [SMEM] * 2 + [VMEM] * 19 + [HBM],
         (
             me_s,
             count_all,
             own,
             other,
-            *ready[:6],
-            memory_now,
+            *ready,
             w_msg,
             w_in,
             touched,
             *late,
-            *stay((*keeps, *snap)),
+            *keeps,
+            *stay(snap),
         ),
         out_specs=(HBM,) * 2,
         scratch_shapes=[
-            pltpu.VMEM((slots, DM), BF16),
-            pltpu.VMEM((touch, DM), BF16),
             pltpu.VMEM((rows, DM), F32),
             pltpu.VMEM((events, DM), BF16),
-            pltpu.SemaphoreType.DMA((2,)),
-            pltpu.SemaphoreType.DMA((2,)),
+            pltpu.SemaphoreType.DMA((3,)),
         ],
         input_output_aliases={21: 1},
     )

time: 194 us -> 194 us (level)
  blocking collectives: 93.7 us -> 96.9 us
    all_to_all x2, waiting for transfers between devices: 6.87 us -> 3.55 us  [body(): lax.all_to_all(served.reshape(shards, part, DM), 'node', split_axis=0, co...]
    all_to_all x6, blocking collectives: 93.7 us -> 96.9 us  [body(): lax.all_to_all(served.reshape(shards, part, DM), 'node', split_axis=0, co...]
    pallas_call x20 -> x21, Pallas kernels: 44.3 us -> 44.5 us  [call(): pl.pallas_call(kernel, out_shape=outs, in_specs=ins, compiler_params=para...]
  transfers between devices with their start and end apart: 11 -> 11, of which waited for: 2 -> 3; matrix products, arithmetic and copies ran while one was open for 2% -> 2% of each run, Pallas kernels for 17% -> 16%
where the time goes in v1:
time: 194 us; the launch traced here: 193 us
  blocking collectives  96.9 us (50%)
  Pallas kernels  47 us (24%)
  starting transfers between devices  37.8 us (19%)
  waiting for transfers between devices  5.36 us (3%)
  local copies, waits for them, and re-layouts  4.08 us (2%)
  between operations  2 us (1%)
    all_to_all x6, blocking collectives, body(): lax.all_to_all(served.reshape(shards, part, DM), 'node', split_axis=0, co...  96.9 us
    pallas_call x21, Pallas kernels, call(): pl.pallas_call(kernel, out_shape=outs, in_specs=ins, compiler_params=para...  44.5 us
    all_to_all x2, starting transfers between devices, body(): lax.all_to_all(served.reshape(shards, part, DM), 'node', split_axis=0, co...  16.1 us
    ppermute x8, starting transfers between devices, body(): other = lax.ppermute(own, 'tm', swap)  15.1 us
    all_to_all x1, starting transfers between devices, body(): lax.all_to_all(packed, 'tm', split_axis=0, concat_axis=0, tiled=True)  6.52 us
  transfers between devices with their start and end apart: 11, of which 3 were waited for; matrix products, arithmetic and copies ran while one was open for 2% of the time, Pallas kernels for 16%

profile of v1, /device:TPU:1, one launch (start us, length us, event | category | flops | bytes accessed | tf_op | source)
XLA Modules:
  0.0 193.4 jit_solution(5576556221768723140)
XLA Ops:
  2.8 6.5 %all-to-all-start = ((s32[8,24,128]{2,1,0:T(8,128)}), s32[8,24,128]{2,1,0:T(8,128)S(1)}, u32[]{:S(2)}, u32[]{:S(2)}) async-start(s32[8,24,128]{2,1,0:T(8,128)} %pack.1), calls=%async_computation | async-start | bytes 196608 | tf_op jit(solution)/shard_map/all_to_all | solution.py:432
  12.5 1.8 all-to-all-done
  16.1 10.5 %all-to-all-start.1 = ((bf16[32,16,256]{2,1,0:T(8,128)(2,1)}), bf16[32,16,256]{2,1,0:T(8,128)(2,1)S(1)}, u32[]{:S(2)}, u32[]{:S(2)}) async-start(bf16[32,16,256]{2,1,0:T(8,128)(2,1)} %bitcast.8), calls=%async_computation.1 | async-start | bytes 524288 | tf_op jit(solution)/shard_map/all_to_all | solution.py:515
  26.6 1.8 table.1
  28.6 6.7 %links.2 = (bf16[5,256,1024]{2,1,0:T(8,128)(2,1)}, bf16[5,256,256]{2,1,0:T(8,128)(2,1)}, f32[5,256,128]{2,1,0:T(8,128)}) custom-call(f32[512,256]{1,0:T(8,128)} %after_ref.1, s32[8,512]{1,0:T(8,128)S(1)} %get-tuple-element.210.src_ref, s32[8,512]{1,0:T(8,128)S(1)} %get-tuple-element.209.dst_ref, s32[8,512]{1,0:T(8,128)S(1)} %get-tuple-element.208.gap_ref, ...), custom_call_target="tpu_custom_call" | custom-call | flops 1000000000 | bytes 4194304 | tf_op jit(solution)/shard_map/links/pallas_call | solution.py:461
  35.3 2.5 %all-to-all-done.1 = bf16[32,16,256]{2,1,0:T(8,128)(2,1)S(1)} async-done(((bf16[32,16,256]{2,1,0:T(8,128)(2,1)}), bf16[32,16,256]{2,1,0:T(8,128)(2,1)S(1)}, u32[]{:S(2)}, u32[]{:S(2)}) %all-to-all-start.1) | async-done | bytes 262176 | tf_op jit(solution)/shard_map/all_to_all | solution.py:515
  37.8 2.5 %collective-permute-start = (bf16[512,256]{1,0:T(8,128)(2,1)S(1)}, bf16[512,256]{1,0:T(8,128)(2,1)S(1)}, u32[]{:S(2)}, u32[]{:S(2)}) collective-permute-start(bf16[512,256]{1,0:T(8,128)(2,1)S(1)} %tie.2.own_ref), channel_id=1, source_target_pairs={{0,32},{32,0},{64,96},{96,64},{128,160},{160,128},{192,224},{224,1... | collective-permute-start | bytes 786440 | tf_op jit(solution)/shard_map/ppermute | solution.py:547
  40.3 2.0 %ready.8 = (f32[256,256]{1,0:T(8,128)S(1)}, f32[256,128]{1,0:T(8,128)S(1)}, bf16[256,512]{1,0:T(8,128)(2,1)S(1)}, f32[256,256]{1,0:T(8,128)S(1)}, f32[256,768]{1...) custom-call(s32[1]{0:T(128)} %bitcast.me_ref, bf16[512,256]{1,0:T(8,128)(2,1)S(1)} %tie.2.own_ref, ...), custom_call_target="tpu_custom_call" | custom-call | flops 1000000000 | bytes 4194304 | tf_op jit(solution)/shard_map/ready/pallas_call | solution.py:461
  42.4 2.0 %update.7 = (bf16[512,256]{1,0:T(8,128)(2,1)}, bf16[512,256]{1,0:T(8,128)(2,1)}, bf16[1024,256]{1,0:T(8,128)(2,1)}, bf16[256,256]{1,0:T(8,128)(2,1)}) custom-call(s32[1]{0:T(128)} %bitcast.me_ref, bf16[512,256]{1,0:T(8,128)(2,1)S(1)} %tie.2.own_ref, bf16[512,256]{1,0:T(8,128)(2,1)S(1)} %collective-permute-done.other_ref, ...), custom_call_target="tpu_custom_call" | custom-call | flops 1000000000 | bytes 4194304 | tf_op jit(solution)/shard_map/update/pallas_call | solution.py:461
  44.4 5.6 %all-to-all-start.2 = ((bf16[32,16,256]{2,1,0:T(8,128)(2,1)}), bf16[32,16,256]{2,1,0:T(8,128)(2,1)S(1)}, u32[]{:S(2)}, u32[]{:S(2)}) async-start(bf16[32,16,256]{2,1,0:T(8,128)(2,1)} %bitcast.12), calls=%async_computation.2 | async-start | bytes 524288 | tf_op jit(solution)/shard_map/all_to_all | solution.py:515
  50.3 4.5 %links.3 = (bf16[3,256,1024]{2,1,0:T(8,128)(2,1)}, bf16[3,256,256]{2,1,0:T(8,128)(2,1)}, f32[3,256,128]{2,1,0:T(8,128)}) custom-call(bf16[512,256]{1,0:T(8,128)(2,1)} %get-tuple-element.119.after_ref.memory_ref, s32[8,512]{1,0:T(8,128)S(1)} %get-tuple-element.210.src_ref, s32[8,512]{1,0:T(8,128)S(1)} %get-tuple-element.209.dst_ref, ...), custom_call_target="tpu_custom_call" | custom-call | flops 1000000000 | bytes 4194304 | tf_op jit(solution)/shard_map/links/pallas_call | solution.py:461
  54.8 2.6 %neighbour_counts.1.refs_1_.nbr_ref = bf16[512,1024]{1,0:T(8,128)(2,1)} custom-call(bf16[512,256]{1,0:T(8,128)(2,1)} %get-tuple-element.119.after_ref.memory_ref, s32[512,21]{1,0:T(8,128)S(1)} %bitcast.115), custom_call_target="tpu_custom_call" | custom-call | flops 1000000000 | bytes 4194304 | tf_op jit(solution)/shard_map/neighbour_counts/pallas_call | solution.py:461
  57.4 2.8 %codes.1.refs_2_.codes_ref = bf16[512,128]{1,0:T(8,128)(2,1)} custom-call(bf16[512,256]{1,0:T(8,128)(2,1)} %get-tuple-element.119.after_ref.memory_ref, s32[512,21]{1,0:T(8,128)S(1)} %bitcast.116, bf16[1024,128]{1,0:T(8,128)(2,1)S(1)} %get-tuple-element.106.table_ref.high_ref, bf16[1024,128]{1,0:T(8,128)(2,1)S(1)} %get-tuple-element.120.low_ref), custom_call_target="tpu_custom_call" | custom-call | flops 1000000000 | bytes 4194304 | tf_op jit(solution)/shard_map/codes/pallas_call | solution.py:461
  61.3 2.5 %collective-permute-start.1 = (bf16[512,256]{1,0:T(8,128)(2,1)S(1)}, bf16[512,256]{1,0:T(8,128)(2,1)S(1)}, u32[]{:S(2)}, u32[]{:S(2)}) collective-permute-start(bf16[512,256]{1,0:T(8,128)(2,1)S(1)} %tie.3.own_ref), channel_id=1, source_target_pairs={{0,32},{32,0},{64,96},{96,64},{128,160},{160,128},{192,224},{224,1... | collective-permute-start | bytes 786440 | tf_op jit(solution)/shard_map/ppermute | solution.py:547
  63.7 1.5 ready.9
  65.2 1.9 update.8
  67.2 19.7 %all_to_all.45 = bf16[32,16,256]{2,1,0:T(8,128)(2,1)S(1)} all-to-all(bf16[32,16,256]{2,1,0:T(8,128)(2,1)S(1)} %bitcast.119), channel_id=1, replica_groups=mesh['tm'=8,'node'=32] {'node'}, dimensions={0} | all-to-all | bytes 524288 | tf_op jit(solution)/shard_map/all_to_all | solution.py:515
  87.3 1.5 ready.10
  90.1 16.0 %all_to_all.46 = bf16[32,16,256]{2,1,0:T(8,128)(2,1)S(1)} all-to-all(bf16[32,16,256]{2,1,0:T(8,128)(2,1)S(1)} %bitcast.120), channel_id=1, replica_groups=mesh['tm'=8,'node'=32] {'node'}, dimensions={0} | all-to-all | bytes 524288 | tf_op jit(solution)/shard_map/all_to_all | solution.py:515
  106.1 1.9 collective-permute-start.3
  108.0 1.5 ready.11
  110.8 15.3 %all_to_all.47 = bf16[32,16,256]{2,1,0:T(8,128)(2,1)S(1)} all-to-all(bf16[32,16,256]{2,1,0:T(8,128)(2,1)S(1)} %bitcast.121), channel_id=1, replica_groups=mesh['tm'=8,'node'=32] {'node'}, dimensions={0} | all-to-all | bytes 524288 | tf_op jit(solution)/shard_map/all_to_all | solution.py:515
  126.0 2.0 %collective-permute-start.4 = (bf16[512,256]{1,0:T(8,128)(2,1)S(1)}, bf16[512,256]{1,0:T(8,128)(2,1)S(1)}, u32[]{:S(2)}, u32[]{:S(2)}) collective-permute-start(bf16[512,256]{1,0:T(8,128)(2,1)S(1)} %bitcast.96), channel_id=1, source_target_pairs={{0,32},{32,0},{64,96},{96,64},{128,160},{160,128},{192,224},{224,1... | collective-permute-start | bytes 786440 | tf_op jit(solution)/shard_map/ppermute | solution.py:547
  130.8 15.3 %all_to_all.48 = bf16[32,16,256]{2,1,0:T(8,128)(2,1)S(1)} all-to-all(bf16[32,16,256]{2,1,0:T(8,128)(2,1)S(1)} %bitcast.122), channel_id=1, replica_groups=mesh['tm'=8,'node'=32] {'node'}, dimensions={0} | all-to-all | bytes 524288 | tf_op jit(solution)/shard_map/all_to_all | solution.py:515
  146.1 2.0 %collective-permute-start.5 = (bf16[512,256]{1,0:T(8,128)(2,1)S(1)}, bf16[512,256]{1,0:T(8,128)(2,1)S(1)}, u32[]{:S(2)}, u32[]{:S(2)}) collective-permute-start(bf16[512,256]{1,0:T(8,128)(2,1)S(1)} %bitcast.99), channel_id=1, source_target_pairs={{0,32},{32,0},{64,96},{96,64},{128,160},{160,128},{192,224},{224,1... | collective-permute-start | bytes 786440 | tf_op jit(solution)/shard_map/ppermute | solution.py:547
  148.1 1.5 ready.13
  150.8 15.3 %all_to_all.49 = bf16[32,16,256]{2,1,0:T(8,128)(2,1)S(1)} all-to-all(bf16[32,16,256]{2,1,0:T(8,128)(2,1)S(1)} %bitcast.123), channel_id=1, replica_groups=mesh['tm'=8,'node'=32] {'node'}, dimensions={0} | all-to-all | bytes 524288 | tf_op jit(solution)/shard_map/all_to_all | solution.py:515
  166.1 2.0 %collective-permute-start.6 = (bf16[512,256]{1,0:T(8,128)(2,1)S(1)}, bf16[512,256]{1,0:T(8,128)(2,1)S(1)}, u32[]{:S(2)}, u32[]{:S(2)}) collective-permute-start(bf16[512,256]{1,0:T(8,128)(2,1)S(1)} %bitcast.102), channel_id=1, source_target_pairs={{0,32},{32,0},{64,96},{96,64},{128,160},{160,128},{192,224},{224,1... | collective-permute-start | bytes 786440 | tf_op jit(solution)/shard_map/ppermute | solution.py:547
  171.0 15.4 %all_to_all.50 = bf16[32,16,256]{2,1,0:T(8,128)(2,1)S(1)} all-to-all(bf16[32,16,256]{2,1,0:T(8,128)(2,1)S(1)} %bitcast.118), channel_id=1, replica_groups=mesh['tm'=8,'node'=32] {'node'}, dimensions={0} | all-to-all | bytes 524288 | tf_op jit(solution)/shard_map/all_to_all | solution.py:515
  186.4 2.0 %collective-permute-start.7 = (bf16[512,256]{1,0:T(8,128)(2,1)S(1)}, bf16[512,256]{1,0:T(8,128)(2,1)S(1)}, u32[]{:S(2)}, u32[]{:S(2)}) collective-permute-start(bf16[512,256]{1,0:T(8,128)(2,1)S(1)} %bitcast.112), channel_id=1, source_target_pairs={{0,32},{32,0},{64,96},{96,64},{128,160},{160,128},{192,224},{224,1... | collective-permute-start | bytes 786440 | tf_op jit(solution)/shard_map/ppermute | solution.py:547
  188.4 1.5 ready.15
  189.9 3.2 %last.1 = (bf16[512,256]{1,0:T(8,128)(2,1)}, f32[512,256]{1,0:T(8,128)}) custom-call(s32[1]{0:T(128)} %bitcast.me_ref, s32[8]{0:T(128)S(1)} %slice_reduce_fusion.count_ref.counts_ref, bf16[512,256]{1,0:T(8,128)(2,1)S(1)} %bitcast.114, bf16[512,256]{1,0:T(8,128)(2,1)S(1)} %collective-permute-done.7.other_ref, ...), custom_call_target="tpu_custom_call", output_to_operand_aliasing={{1}: (21, {})} | custom-call | flops 1000000000 | bytes 4194304 | tf_op jit(solution)/shard_map/last/pallas_call | solution.py:461
  (63 shorter events, 17.6 us)
Async XLA Ops:
  0.6 14.4 %copy-start.6 = (f32[512,256]{1,0:T(8,128)S(1)}, f32[512,256]{1,0:T(8,128)}, u32[]{:S(2)}) copy-start(f32[512,256]{1,0:T(8,128)} %after_ref.1) | copy-start | bytes 1572868
  2.8 11.5 %all-to-all-start = ((s32[8,24,128]{2,1,0:T(8,128)}), s32[8,24,128]{2,1,0:T(8,128)S(1)}, u32[]{:S(2)}, u32[]{:S(2)}) async-start(s32[8,24,128]{2,1,0:T(8,128)} %pack.1), calls=%async_computation | async-start | bytes 196608 | tf_op jit(solution)/shard_map/all_to_all | solution.py:432
  16.1 21.7 %all-to-all-start.1 = ((bf16[32,16,256]{2,1,0:T(8,128)(2,1)}), bf16[32,16,256]{2,1,0:T(8,128)(2,1)S(1)}, u32[]{:S(2)}, u32[]{:S(2)}) async-start(bf16[32,16,256]{2,1,0:T(8,128)(2,1)} %bitcast.8), calls=%async_computation.1 | async-start | bytes 524288 | tf_op jit(solution)/shard_map/all_to_all | solution.py:515
  28.6 11.7 %copy-start.10 = (s32[1,1,10,512]{3,1,2,0:T(1,128)S(1)}, s32[1,1,10,512]{3,1,2,0:T(1,128)}, u32[]{:S(2)}) copy-start(s32[1,1,10,512]{3,1,2,0:T(1,128)} %param.24) | copy-start | bytes 61444
  28.6 11.7 %copy-start.1 = (bf16[256,768]{1,0:T(8,128)(2,1)S(1)}, bf16[256,768]{1,0:T(8,128)(2,1)}, u32[]{:S(2)}) copy-start(bf16[256,768]{1,0:T(8,128)(2,1)} %w_hid_ref.15) | copy-start | bytes 1179652
  37.8 4.5 %collective-permute-start = (bf16[512,256]{1,0:T(8,128)(2,1)S(1)}, bf16[512,256]{1,0:T(8,128)(2,1)S(1)}, u32[]{:S(2)}, u32[]{:S(2)}) collective-permute-start(bf16[512,256]{1,0:T(8,128)(2,1)S(1)} %tie.2.own_ref), channel_id=1, source_target_pairs={{0,32},{32,0},{64,96},{96,64},{128,160},{160,128},{192,224},{224,1... | collective-permute-start | bytes 786440 | tf_op jit(solution)/shard_map/ppermute | solution.py:547
  40.3 2.1 %copy-start.2 = (bf16[256,768]{1,0:T(8,128)(2,1)S(1)}, bf16[256,768]{1,0:T(8,128)(2,1)}, u32[]{:S(2)}) copy-start(bf16[256,768]{1,0:T(8,128)(2,1)} %w_in_ref.15) | copy-start | bytes 1179652
  42.3 7.7 %copy-start.11 = (s32[1,1,10,512]{3,1,2,0:T(1,128)S(1)}, s32[1,1,10,512]{3,1,2,0:T(1,128)}, u32[]{:S(2)}) copy-start(s32[1,1,10,512]{3,1,2,0:T(1,128)} %param.22) | copy-start | bytes 61444
  42.3 7.8 %copy-start.12 = (s32[1,1,512]{2,1,0:T(1,128)S(1)}, s32[1,1,512]{2,1,0:T(1,128)}, u32[]{:S(2)}) copy-start(s32[1,1,512]{2,1,0:T(1,128)} %param.18) | copy-start | bytes 6148
  44.4 16.8 %all-to-all-start.2 = ((bf16[32,16,256]{2,1,0:T(8,128)(2,1)}), bf16[32,16,256]{2,1,0:T(8,128)(2,1)S(1)}, u32[]{:S(2)}, u32[]{:S(2)}) async-start(bf16[32,16,256]{2,1,0:T(8,128)(2,1)} %bitcast.12), calls=%async_computation.2 | async-start | bytes 524288 | tf_op jit(solution)/shard_map/all_to_all | solution.py:515
  57.4 6.3 %copy-start.7 = (bf16[512,256]{1,0:T(8,128)(2,1)S(1)}, bf16[512,256]{1,0:T(8,128)(2,1)}, u32[]{:S(2)}) copy-start(bf16[512,256]{1,0:T(8,128)(2,1)} %get-tuple-element.119.after_ref.memory_ref) | copy-start | bytes 786436
  61.3 4.0 %collective-permute-start.1 = (bf16[512,256]{1,0:T(8,128)(2,1)S(1)}, bf16[512,256]{1,0:T(8,128)(2,1)S(1)}, u32[]{:S(2)}, u32[]{:S(2)}) collective-permute-start(bf16[512,256]{1,0:T(8,128)(2,1)S(1)} %tie.3.own_ref), channel_id=1, source_target_pairs={{0,32},{32,0},{64,96},{96,64},{128,160},{160,128},{192,224},{224,1... | collective-permute-start | bytes 786440 | tf_op jit(solution)/shard_map/ppermute | solution.py:547
  86.9 1.9 %collective-permute-start.2 = (bf16[512,256]{1,0:T(8,128)(2,1)S(1)}, bf16[512,256]{1,0:T(8,128)(2,1)S(1)}, u32[]{:S(2)}, u32[]{:S(2)}) collective-permute-start(bf16[512,256]{1,0:T(8,128)(2,1)S(1)} %bitcast.105), channel_id=1, source_target_pairs={{0,32},{32,0},{64,96},{96,64},{128,160},{160,128},{192,224},{224,1... | collective-permute-start | bytes 786440 | tf_op jit(solution)/shard_map/ppermute | solution.py:547
  106.1 3.4 %collective-permute-start.3 = (bf16[512,256]{1,0:T(8,128)(2,1)S(1)}, bf16[512,256]{1,0:T(8,128)(2,1)S(1)}, u32[]{:S(2)}, u32[]{:S(2)}) collective-permute-start(bf16[512,256]{1,0:T(8,128)(2,1)S(1)} %bitcast.108), channel_id=1, source_target_pairs={{0,32},{32,0},{64,96},{96,64},{128,160},{160,128},{192,224},{224,1... | collective-permute-start | bytes 786440 | tf_op jit(solution)/shard_map/ppermute | solution.py:547
  126.0 3.5 %collective-permute-start.4 = (bf16[512,256]{1,0:T(8,128)(2,1)S(1)}, bf16[512,256]{1,0:T(8,128)(2,1)S(1)}, u32[]{:S(2)}, u32[]{:S(2)}) collective-permute-start(bf16[512,256]{1,0:T(8,128)(2,1)S(1)} %bitcast.96), channel_id=1, source_target_pairs={{0,32},{32,0},{64,96},{96,64},{128,160},{160,128},{192,224},{224,1... | collective-permute-start | bytes 786440 | tf_op jit(solution)/shard_map/ppermute | solution.py:547
  146.1 3.5 %collective-permute-start.5 = (bf16[512,256]{1,0:T(8,128)(2,1)S(1)}, bf16[512,256]{1,0:T(8,128)(2,1)S(1)}, u32[]{:S(2)}, u32[]{:S(2)}) collective-permute-start(bf16[512,256]{1,0:T(8,128)(2,1)S(1)} %bitcast.99), channel_id=1, source_target_pairs={{0,32},{32,0},{64,96},{96,64},{128,160},{160,128},{192,224},{224,1... | collective-permute-start | bytes 786440 | tf_op jit(solution)/shard_map/ppermute | solution.py:547
  166.1 3.5 %collective-permute-start.6 = (bf16[512,256]{1,0:T(8,128)(2,1)S(1)}, bf16[512,256]{1,0:T(8,128)(2,1)S(1)}, u32[]{:S(2)}, u32[]{:S(2)}) collective-permute-start(bf16[512,256]{1,0:T(8,128)(2,1)S(1)} %bitcast.102), channel_id=1, source_target_pairs={{0,32},{32,0},{64,96},{96,64},{128,160},{160,128},{192,224},{224,1... | collective-permute-start | bytes 786440 | tf_op jit(solution)/shard_map/ppermute | solution.py:547
  169.6 18.7 %copy-start.9 = (bf16[356,256]{1,0:T(8,128)(2,1)S(1)}, bf16[356,256]{1,0:T(8,128)(2,1)}, u32[]{:S(2)}) copy-start(bf16[356,256]{1,0:T(8,128)(2,1)} %param.30) | copy-start | bytes 546820
  170.9 19.0 %copy-start = (bf16[1024,256]{1,0:T(8,128)(2,1)S(1)}, bf16[1024,256]{1,0:T(8,128)(2,1)}, u32[]{:S(2)}) copy-start(bf16[1024,256]{1,0:T(8,128)(2,1)} %get-tuple-element.203.rows_ref) | copy-start | bytes 1572868
  170.9 19.0 %copy-start.3 = (bf16[256,256]{1,0:T(8,128)(2,1)S(1)}, bf16[256,256]{1,0:T(8,128)(2,1)}, u32[]{:S(2)}) copy-start(bf16[256,256]{1,0:T(8,128)(2,1)} %get-tuple-element.204.fresh_kept_ref) | copy-start | bytes 393220
  170.9 19.0 %copy-start.4 = (bf16[512,1024]{1,0:T(8,128)(2,1)S(1)}, bf16[512,1024]{1,0:T(8,128)(2,1)}, u32[]{:S(2)}) copy-start(bf16[512,1024]{1,0:T(8,128)(2,1)} %neighbour_counts.1.refs_1_.nbr_ref) | copy-start | bytes 3145732
  170.9 19.0 %copy-start.5 = (bf16[512,128]{1,0:T(8,128)(2,1)S(1)}, bf16[512,128]{1,0:T(8,128)(2,1)}, u32[]{:S(2)}) copy-start(bf16[512,128]{1,0:T(8,128)(2,1)} %codes.1.refs_2_.codes_ref) | copy-start | bytes 393220
  170.9 19.0 %copy-start.8 = (bf16[512,256]{1,0:T(8,128)(2,1)S(1)}, bf16[512,256]{1,0:T(8,128)(2,1)}, u32[]{:S(2)}) copy-start(bf16[512,256]{1,0:T(8,128)(2,1)} %w_out_ref.1) | copy-start | bytes 786436
  186.4 3.5 %collective-permute-start.7 = (bf16[512,256]{1,0:T(8,128)(2,1)S(1)}, bf16[512,256]{1,0:T(8,128)(2,1)S(1)}, u32[]{:S(2)}, u32[]{:S(2)}) collective-permute-start(bf16[512,256]{1,0:T(8,128)(2,1)S(1)} %bitcast.112), channel_id=1, source_target_pairs={{0,32},{32,0},{64,96},{96,64},{128,160},{160,128},{192,224},{224,1... | collective-permute-start | bytes 786440 | tf_op jit(solution)/shard_map/ppermute | solution.py:547

commit v2 on v1

--- a/solution.py
+++ b/solution.py
@@ -12,7 +12,7 @@
 CODE = 128
 GAPS = 1024
 NBRS = 10
-FIRST = 5
+FIRST = 6
 F32 = jnp.float32
 BF16 = jnp.bfloat16
 VMEM = pl.BlockSpec(memory_space=pltpu.VMEM)
@@ -479,11 +479,11 @@
     served, memory_now = pl.pallas_call(
         first_serve_kernel,
         out_shape=(shape((half, DM), BF16), shape((rows, DM), BF16)),
-        in_specs=[VMEM] * 2 + [ANY] * 2,
+        in_specs=[VMEM] * 2 + [ANY] * 4,
         out_specs=(VMEM,) * 2,
         compiler_params=params(),
         name="first_serve",
-    )(serve_t, memory, touched, touched_t)
+    )(serve_t, memory, touched, touched_t, table, w_msg)
 
     def make_links(begin, number, after):
         return call(

time: 194 us -> 193 us (level)
  transfers between devices with their start and end apart: 11 -> 11, of which waited for: 3 -> 2; matrix products, arithmetic and copies ran while one was open for 2% -> 2% of each run, Pallas kernels for 16% -> 16%
where the time goes in v2:
time: 193 us; the launch traced here: 192 us
  blocking collectives  95.8 us (50%)
  Pallas kernels  47 us (24%)
  starting transfers between devices  37.1 us (19%)
  waiting for transfers between devices  5.42 us (3%)
  local copies, waits for them, and re-layouts  4.08 us (2%)
  between operations  2 us (1%)
    all_to_all x6, blocking collectives, body(): lax.all_to_all(served.reshape(shards, part, DM), 'node', split_axis=0, co...  95.8 us
    pallas_call x21, Pallas kernels, call(): pl.pallas_call(kernel, out_shape=outs, in_specs=ins, compiler_params=para...  44.5 us
    all_to_all x2, starting transfers between devices, body(): lax.all_to_all(served.reshape(shards, part, DM), 'node', split_axis=0, co...  15.5 us
    ppermute x8, starting transfers between devices, body(): other = lax.ppermute(own, 'tm', swap)  15.1 us
    all_to_all x1, starting transfers between devices, body(): lax.all_to_all(packed, 'tm', split_axis=0, concat_axis=0, tiled=True)  6.52 us
    all_to_all x2, waiting for transfers between devices, body(): lax.all_to_all(served.reshape(shards, part, DM), 'node', split_axis=0, co...  5.39 us
  transfers between devices with their start and end apart: 11, of which 2 were waited for; matrix products, arithmetic and copies ran while one was open for 2% of the time, Pallas kernels for 16%

profile of v2, /device:TPU:1, one launch (start us, length us, event | category | flops | bytes accessed | tf_op | source)
XLA Modules:
  0.0 191.6 jit_solution(10154682837516353814)
XLA Ops:
  2.8 6.5 %all-to-all-start = ((s32[8,24,128]{2,1,0:T(8,128)}), s32[8,24,128]{2,1,0:T(8,128)S(1)}, u32[]{:S(2)}, u32[]{:S(2)}) async-start(s32[8,24,128]{2,1,0:T(8,128)} %pack.1), calls=%async_computation | async-start | bytes 196608 | tf_op jit(solution)/shard_map/all_to_all | solution.py:432
  12.5 1.8 table.1
  16.1 10.5 %all-to-all-start.1 = ((bf16[32,16,256]{2,1,0:T(8,128)(2,1)}), bf16[32,16,256]{2,1,0:T(8,128)(2,1)S(1)}, u32[]{:S(2)}, u32[]{:S(2)}) async-start(bf16[32,16,256]{2,1,0:T(8,128)(2,1)} %bitcast.10), calls=%async_computation.1 | async-start | bytes 524288 | tf_op jit(solution)/shard_map/all_to_all | solution.py:515
  26.8 7.8 %links.2 = (bf16[6,256,1024]{2,1,0:T(8,128)(2,1)}, bf16[6,256,256]{2,1,0:T(8,128)(2,1)}, f32[6,256,128]{2,1,0:T(8,128)}) custom-call(f32[512,256]{1,0:T(8,128)} %after_ref.1, s32[8,512]{1,0:T(8,128)S(1)} %get-tuple-element.210.src_ref, s32[8,512]{1,0:T(8,128)S(1)} %get-tuple-element.209.dst_ref, s32[8,512]{1,0:T(8,128)S(1)} %get-tuple-element.208.gap_ref, ...), custom_call_target="tpu_custom_call" | custom-call | flops 1000000000 | bytes 4194304 | tf_op jit(solution)/shard_map/links/pallas_call | solution.py:461
  34.6 3.3 %all-to-all-done.1 = bf16[32,16,256]{2,1,0:T(8,128)(2,1)S(1)} async-done(((bf16[32,16,256]{2,1,0:T(8,128)(2,1)}), bf16[32,16,256]{2,1,0:T(8,128)(2,1)S(1)}, u32[]{:S(2)}, u32[]{:S(2)}) %all-to-all-start.1) | async-done | bytes 262176 | tf_op jit(solution)/shard_map/all_to_all | solution.py:515
  37.9 2.4 %collective-permute-start = (bf16[512,256]{1,0:T(8,128)(2,1)S(1)}, bf16[512,256]{1,0:T(8,128)(2,1)S(1)}, u32[]{:S(2)}, u32[]{:S(2)}) collective-permute-start(bf16[512,256]{1,0:T(8,128)(2,1)S(1)} %tie.2.own_ref), channel_id=1, source_target_pairs={{0,32},{32,0},{64,96},{96,64},{128,160},{160,128},{192,224},{224,1... | collective-permute-start | bytes 786440 | tf_op jit(solution)/shard_map/ppermute | solution.py:547
  40.3 2.0 %ready.8 = (f32[256,256]{1,0:T(8,128)S(1)}, f32[256,128]{1,0:T(8,128)S(1)}, bf16[256,512]{1,0:T(8,128)(2,1)S(1)}, f32[256,256]{1,0:T(8,128)S(1)}, f32[256,768]{1...) custom-call(s32[1]{0:T(128)} %bitcast.me_ref, bf16[512,256]{1,0:T(8,128)(2,1)S(1)} %tie.2.own_ref, ...), custom_call_target="tpu_custom_call" | custom-call | flops 1000000000 | bytes 4194304 | tf_op jit(solution)/shard_map/ready/pallas_call | solution.py:461
  42.4 2.0 %update.7 = (bf16[512,256]{1,0:T(8,128)(2,1)}, bf16[512,256]{1,0:T(8,128)(2,1)}, bf16[1024,256]{1,0:T(8,128)(2,1)}, bf16[256,256]{1,0:T(8,128)(2,1)}) custom-call(s32[1]{0:T(128)} %bitcast.me_ref, bf16[512,256]{1,0:T(8,128)(2,1)S(1)} %tie.2.own_ref, bf16[512,256]{1,0:T(8,128)(2,1)S(1)} %collective-permute-done.other_ref, ...), custom_call_target="tpu_custom_call" | custom-call | flops 1000000000 | bytes 4194304 | tf_op jit(solution)/shard_map/update/pallas_call | solution.py:461
  44.4 5.0 %all-to-all-start.2 = ((bf16[32,16,256]{2,1,0:T(8,128)(2,1)}), bf16[32,16,256]{2,1,0:T(8,128)(2,1)S(1)}, u32[]{:S(2)}, u32[]{:S(2)}) async-start(bf16[32,16,256]{2,1,0:T(8,128)(2,1)} %bitcast.12), calls=%async_computation.2 | async-start | bytes 524288 | tf_op jit(solution)/shard_map/all_to_all | solution.py:515
  49.7 3.5 %links.3 = (bf16[2,256,1024]{2,1,0:T(8,128)(2,1)}, bf16[2,256,256]{2,1,0:T(8,128)(2,1)}, f32[2,256,128]{2,1,0:T(8,128)}) custom-call(bf16[512,256]{1,0:T(8,128)(2,1)} %get-tuple-element.119.after_ref.memory_ref, s32[8,512]{1,0:T(8,128)S(1)} %get-tuple-element.210.src_ref, s32[8,512]{1,0:T(8,128)S(1)} %get-tuple-element.209.dst_ref, ...), custom_call_target="tpu_custom_call" | custom-call | flops 1000000000 | bytes 4194304 | tf_op jit(solution)/shard_map/links/pallas_call | solution.py:461
  53.1 2.6 %neighbour_counts.1.refs_1_.nbr_ref = bf16[512,1024]{1,0:T(8,128)(2,1)} custom-call(bf16[512,256]{1,0:T(8,128)(2,1)} %get-tuple-element.119.after_ref.memory_ref, s32[512,21]{1,0:T(8,128)S(1)} %bitcast.112), custom_call_target="tpu_custom_call" | custom-call | flops 1000000000 | bytes 4194304 | tf_op jit(solution)/shard_map/neighbour_counts/pallas_call | solution.py:461
  55.7 2.8 %codes.1.refs_2_.codes_ref = bf16[512,128]{1,0:T(8,128)(2,1)} custom-call(bf16[512,256]{1,0:T(8,128)(2,1)} %get-tuple-element.119.after_ref.memory_ref, s32[512,21]{1,0:T(8,128)S(1)} %bitcast.113, bf16[1024,128]{1,0:T(8,128)(2,1)S(1)} %get-tuple-element.105.rest_2_.table_ref.high_ref, bf16[1024,128]{1,0:T(8,128)(2,1)S(1)} %get-tuple-element.120.low_ref), custom_call_target="tpu_custom_call" | custom-call | flops 1000000000 | bytes 4194304 | tf_op jit(solution)/shard_map/codes/pallas_call | solution.py:461
  58.5 2.1 %all-to-all-done.2 = bf16[32,16,256]{2,1,0:T(8,128)(2,1)S(1)} async-done(((bf16[32,16,256]{2,1,0:T(8,128)(2,1)}), bf16[32,16,256]{2,1,0:T(8,128)(2,1)S(1)}, u32[]{:S(2)}, u32[]{:S(2)}) %all-to-all-start.2) | async-done | bytes 262176 | tf_op jit(solution)/shard_map/all_to_all | solution.py:515
  60.6 2.4 %collective-permute-start.1 = (bf16[512,256]{1,0:T(8,128)(2,1)S(1)}, bf16[512,256]{1,0:T(8,128)(2,1)S(1)}, u32[]{:S(2)}, u32[]{:S(2)}) collective-permute-start(bf16[512,256]{1,0:T(8,128)(2,1)S(1)} %tie.3.own_ref), channel_id=1, source_target_pairs={{0,32},{32,0},{64,96},{96,64},{128,160},{160,128},{192,224},{224,1... | collective-permute-start | bytes 786440 | tf_op jit(solution)/shard_map/ppermute | solution.py:547
  63.1 1.5 ready.9
  64.6 1.9 %update.8 = (bf16[512,256]{1,0:T(8,128)(2,1)S(1)}, bf16[512,256]{1,0:T(8,128)(2,1)S(1)}, bf16[1024,256]{1,0:T(8,128)(2,1)}, bf16[256,256]{1,0:T(8,128)(2,1)}) custom-call(s32[1]{0:T(128)} %bitcast.me_ref, bf16[512,256]{1,0:T(8,128)(2,1)S(1)} %tie.3.own_ref, ...), custom_call_target="tpu_custom_call", output_to_operand_aliasing={{2}: (14, {}), {3}: (15, {})} | custom-call | flops 1000000000 | bytes 4194304 | tf_op jit(solution)/shard_map/update/pallas_call | solution.py:461
  66.5 18.6 %all_to_all.45 = bf16[32,16,256]{2,1,0:T(8,128)(2,1)S(1)} all-to-all(bf16[32,16,256]{2,1,0:T(8,128)(2,1)S(1)} %bitcast.119), channel_id=1, replica_groups=mesh['tm'=8,'node'=32] {'node'}, dimensions={0} | all-to-all | bytes 524288 | tf_op jit(solution)/shard_map/all_to_all | solution.py:515
  85.5 1.5 ready.10
  88.4 16.0 %all_to_all.46 = bf16[32,16,256]{2,1,0:T(8,128)(2,1)S(1)} all-to-all(bf16[32,16,256]{2,1,0:T(8,128)(2,1)S(1)} %bitcast.120), channel_id=1, replica_groups=mesh['tm'=8,'node'=32] {'node'}, dimensions={0} | all-to-all | bytes 524288 | tf_op jit(solution)/shard_map/all_to_all | solution.py:515
  104.3 1.9 collective-permute-start.3
  106.2 1.5 ready.11
  109.0 15.3 %all_to_all.47 = bf16[32,16,256]{2,1,0:T(8,128)(2,1)S(1)} all-to-all(bf16[32,16,256]{2,1,0:T(8,128)(2,1)S(1)} %bitcast.121), channel_id=1, replica_groups=mesh['tm'=8,'node'=32] {'node'}, dimensions={0} | all-to-all | bytes 524288 | tf_op jit(solution)/shard_map/all_to_all | solution.py:515
  124.3 2.0 %collective-permute-start.4 = (bf16[512,256]{1,0:T(8,128)(2,1)S(1)}, bf16[512,256]{1,0:T(8,128)(2,1)S(1)}, u32[]{:S(2)}, u32[]{:S(2)}) collective-permute-start(bf16[512,256]{1,0:T(8,128)(2,1)S(1)} %bitcast.89), channel_id=1, source_target_pairs={{0,32},{32,0},{64,96},{96,64},{128,160},{160,128},{192,224},{224,1... | collective-permute-start | bytes 786440 | tf_op jit(solution)/shard_map/ppermute | solution.py:547
  129.1 15.3 %all_to_all.48 = bf16[32,16,256]{2,1,0:T(8,128)(2,1)S(1)} all-to-all(bf16[32,16,256]{2,1,0:T(8,128)(2,1)S(1)} %bitcast.122), channel_id=1, replica_groups=mesh['tm'=8,'node'=32] {'node'}, dimensions={0} | all-to-all | bytes 524288 | tf_op jit(solution)/shard_map/all_to_all | solution.py:515
  144.4 2.0 %collective-permute-start.5 = (bf16[512,256]{1,0:T(8,128)(2,1)S(1)}, bf16[512,256]{1,0:T(8,128)(2,1)S(1)}, u32[]{:S(2)}, u32[]{:S(2)}) collective-permute-start(bf16[512,256]{1,0:T(8,128)(2,1)S(1)} %bitcast.80), channel_id=1, source_target_pairs={{0,32},{32,0},{64,96},{96,64},{128,160},{160,128},{192,224},{224,1... | collective-permute-start | bytes 786440 | tf_op jit(solution)/shard_map/ppermute | solution.py:547
  149.1 15.3 %all_to_all.49 = bf16[32,16,256]{2,1,0:T(8,128)(2,1)S(1)} all-to-all(bf16[32,16,256]{2,1,0:T(8,128)(2,1)S(1)} %bitcast.123), channel_id=1, replica_groups=mesh['tm'=8,'node'=32] {'node'}, dimensions={0} | all-to-all | bytes 524288 | tf_op jit(solution)/shard_map/all_to_all | solution.py:515
  164.4 2.0 %collective-permute-start.6 = (bf16[512,256]{1,0:T(8,128)(2,1)S(1)}, bf16[512,256]{1,0:T(8,128)(2,1)S(1)}, u32[]{:S(2)}, u32[]{:S(2)}) collective-permute-start(bf16[512,256]{1,0:T(8,128)(2,1)S(1)} %bitcast.109), channel_id=1, source_target_pairs={{0,32},{32,0},{64,96},{96,64},{128,160},{160,128},{192,224},{224,1... | collective-permute-start | bytes 786440 | tf_op jit(solution)/shard_map/ppermute | solution.py:547
  166.4 1.5 ready.14
  169.2 15.4 %all_to_all.50 = bf16[32,16,256]{2,1,0:T(8,128)(2,1)S(1)} all-to-all(bf16[32,16,256]{2,1,0:T(8,128)(2,1)S(1)} %bitcast.118), channel_id=1, replica_groups=mesh['tm'=8,'node'=32] {'node'}, dimensions={0} | all-to-all | bytes 524288 | tf_op jit(solution)/shard_map/all_to_all | solution.py:515
  184.7 2.0 %collective-permute-start.7 = (bf16[512,256]{1,0:T(8,128)(2,1)S(1)}, bf16[512,256]{1,0:T(8,128)(2,1)S(1)}, u32[]{:S(2)}, u32[]{:S(2)}) collective-permute-start(bf16[512,256]{1,0:T(8,128)(2,1)S(1)} %bitcast.115), channel_id=1, source_target_pairs={{0,32},{32,0},{64,96},{96,64},{128,160},{160,128},{192,224},{224,1... | collective-permute-start | bytes 786440 | tf_op jit(solution)/shard_map/ppermute | solution.py:547
  186.6 1.5 ready.15
  188.2 3.2 %last.1 = (bf16[512,256]{1,0:T(8,128)(2,1)}, f32[512,256]{1,0:T(8,128)}) custom-call(s32[1]{0:T(128)} %bitcast.me_ref, s32[8]{0:T(128)S(1)} %slice_reduce_fusion.count_ref.counts_ref, bf16[512,256]{1,0:T(8,128)(2,1)S(1)} %bitcast.117, bf16[512,256]{1,0:T(8,128)(2,1)S(1)} %collective-permute-done.7.other_ref, ...), custom_call_target="tpu_custom_call", output_to_operand_aliasing={{1}: (21, {})} | custom-call | flops 1000000000 | bytes 4194304 | tf_op jit(solution)/shard_map/last/pallas_call | solution.py:461
  (63 shorter events, 16.6 us)
Async XLA Ops:
  0.6 14.5 %copy-start.5 = (f32[512,256]{1,0:T(8,128)S(1)}, f32[512,256]{1,0:T(8,128)}, u32[]{:S(2)}) copy-start(f32[512,256]{1,0:T(8,128)} %after_ref.1) | copy-start | bytes 1572868
  2.8 11.5 %all-to-all-start = ((s32[8,24,128]{2,1,0:T(8,128)}), s32[8,24,128]{2,1,0:T(8,128)S(1)}, u32[]{:S(2)}, u32[]{:S(2)}) async-start(s32[8,24,128]{2,1,0:T(8,128)} %pack.1), calls=%async_computation | async-start | bytes 196608 | tf_op jit(solution)/shard_map/all_to_all | solution.py:432
  16.1 21.7 %all-to-all-start.1 = ((bf16[32,16,256]{2,1,0:T(8,128)(2,1)}), bf16[32,16,256]{2,1,0:T(8,128)(2,1)S(1)}, u32[]{:S(2)}, u32[]{:S(2)}) async-start(bf16[32,16,256]{2,1,0:T(8,128)(2,1)} %bitcast.10), calls=%async_computation.1 | async-start | bytes 524288 | tf_op jit(solution)/shard_map/all_to_all | solution.py:515
  26.8 13.5 %copy-start.10 = (s32[1,1,10,512]{3,1,2,0:T(1,128)S(1)}, s32[1,1,10,512]{3,1,2,0:T(1,128)}, u32[]{:S(2)}) copy-start(s32[1,1,10,512]{3,1,2,0:T(1,128)} %param.24) | copy-start | bytes 61444
  26.8 13.5 %copy-start.2 = (bf16[256,768]{1,0:T(8,128)(2,1)S(1)}, bf16[256,768]{1,0:T(8,128)(2,1)}, u32[]{:S(2)}) copy-start(bf16[256,768]{1,0:T(8,128)(2,1)} %w_hid_ref.15) | copy-start | bytes 1179652
  37.9 4.5 %copy-start.1 = (bf16[256,768]{1,0:T(8,128)(2,1)S(1)}, bf16[256,768]{1,0:T(8,128)(2,1)}, u32[]{:S(2)}) copy-start(bf16[256,768]{1,0:T(8,128)(2,1)} %w_in_ref.15) | copy-start | bytes 1179652
  37.9 4.5 %collective-permute-start = (bf16[512,256]{1,0:T(8,128)(2,1)S(1)}, bf16[512,256]{1,0:T(8,128)(2,1)S(1)}, u32[]{:S(2)}, u32[]{:S(2)}) collective-permute-start(bf16[512,256]{1,0:T(8,128)(2,1)S(1)} %tie.2.own_ref), channel_id=1, source_target_pairs={{0,32},{32,0},{64,96},{96,64},{128,160},{160,128},{192,224},{224,1... | collective-permute-start | bytes 786440 | tf_op jit(solution)/shard_map/ppermute | solution.py:547
  42.3 7.1 %copy-start.11 = (s32[1,1,10,512]{3,1,2,0:T(1,128)S(1)}, s32[1,1,10,512]{3,1,2,0:T(1,128)}, u32[]{:S(2)}) copy-start(s32[1,1,10,512]{3,1,2,0:T(1,128)} %param.22) | copy-start | bytes 61444
  42.4 7.2 %copy-start.12 = (s32[1,1,512]{2,1,0:T(1,128)S(1)}, s32[1,1,512]{2,1,0:T(1,128)}, u32[]{:S(2)}) copy-start(s32[1,1,512]{2,1,0:T(1,128)} %param.18) | copy-start | bytes 6148
  44.4 16.2 %all-to-all-start.2 = ((bf16[32,16,256]{2,1,0:T(8,128)(2,1)}), bf16[32,16,256]{2,1,0:T(8,128)(2,1)S(1)}, u32[]{:S(2)}, u32[]{:S(2)}) async-start(bf16[32,16,256]{2,1,0:T(8,128)(2,1)} %bitcast.12), calls=%async_computation.2 | async-start | bytes 524288 | tf_op jit(solution)/shard_map/all_to_all | solution.py:515
  55.7 7.4 %copy-start.7 = (bf16[512,256]{1,0:T(8,128)(2,1)S(1)}, bf16[512,256]{1,0:T(8,128)(2,1)}, u32[]{:S(2)}) copy-start(bf16[512,256]{1,0:T(8,128)(2,1)} %get-tuple-element.119.after_ref.memory_ref) | copy-start | bytes 786436
  60.6 4.0 %collective-permute-start.1 = (bf16[512,256]{1,0:T(8,128)(2,1)S(1)}, bf16[512,256]{1,0:T(8,128)(2,1)S(1)}, u32[]{:S(2)}, u32[]{:S(2)}) collective-permute-start(bf16[512,256]{1,0:T(8,128)(2,1)S(1)} %tie.3.own_ref), channel_id=1, source_target_pairs={{0,32},{32,0},{64,96},{96,64},{128,160},{160,128},{192,224},{224,1... | collective-permute-start | bytes 786440 | tf_op jit(solution)/shard_map/ppermute | solution.py:547
  85.1 1.9 %collective-permute-start.2 = (bf16[512,256]{1,0:T(8,128)(2,1)S(1)}, bf16[512,256]{1,0:T(8,128)(2,1)S(1)}, u32[]{:S(2)}, u32[]{:S(2)}) collective-permute-start(bf16[512,256]{1,0:T(8,128)(2,1)S(1)} %bitcast.83), channel_id=1, source_target_pairs={{0,32},{32,0},{64,96},{96,64},{128,160},{160,128},{192,224},{224,1... | collective-permute-start | bytes 786440 | tf_op jit(solution)/shard_map/ppermute | solution.py:547
  104.3 3.4 %collective-permute-start.3 = (bf16[512,256]{1,0:T(8,128)(2,1)S(1)}, bf16[512,256]{1,0:T(8,128)(2,1)S(1)}, u32[]{:S(2)}, u32[]{:S(2)}) collective-permute-start(bf16[512,256]{1,0:T(8,128)(2,1)S(1)} %bitcast.86), channel_id=1, source_target_pairs={{0,32},{32,0},{64,96},{96,64},{128,160},{160,128},{192,224},{224,1... | collective-permute-start | bytes 786440 | tf_op jit(solution)/shard_map/ppermute | solution.py:547
  124.3 3.5 %collective-permute-start.4 = (bf16[512,256]{1,0:T(8,128)(2,1)S(1)}, bf16[512,256]{1,0:T(8,128)(2,1)S(1)}, u32[]{:S(2)}, u32[]{:S(2)}) collective-permute-start(bf16[512,256]{1,0:T(8,128)(2,1)S(1)} %bitcast.89), channel_id=1, source_target_pairs={{0,32},{32,0},{64,96},{96,64},{128,160},{160,128},{192,224},{224,1... | collective-permute-start | bytes 786440 | tf_op jit(solution)/shard_map/ppermute | solution.py:547
  144.4 3.5 %collective-permute-start.5 = (bf16[512,256]{1,0:T(8,128)(2,1)S(1)}, bf16[512,256]{1,0:T(8,128)(2,1)S(1)}, u32[]{:S(2)}, u32[]{:S(2)}) collective-permute-start(bf16[512,256]{1,0:T(8,128)(2,1)S(1)} %bitcast.80), channel_id=1, source_target_pairs={{0,32},{32,0},{64,96},{96,64},{128,160},{160,128},{192,224},{224,1... | collective-permute-start | bytes 786440 | tf_op jit(solution)/shard_map/ppermute | solution.py:547
  164.4 3.5 %collective-permute-start.6 = (bf16[512,256]{1,0:T(8,128)(2,1)S(1)}, bf16[512,256]{1,0:T(8,128)(2,1)S(1)}, u32[]{:S(2)}, u32[]{:S(2)}) collective-permute-start(bf16[512,256]{1,0:T(8,128)(2,1)S(1)} %bitcast.109), channel_id=1, source_target_pairs={{0,32},{32,0},{64,96},{96,64},{128,160},{160,128},{192,224},{224,1... | collective-permute-start | bytes 786440 | tf_op jit(solution)/shard_map/ppermute | solution.py:547
  167.9 18.7 %copy-start.9 = (bf16[356,256]{1,0:T(8,128)(2,1)S(1)}, bf16[356,256]{1,0:T(8,128)(2,1)}, u32[]{:S(2)}) copy-start(bf16[356,256]{1,0:T(8,128)(2,1)} %param.30) | copy-start | bytes 546820
  169.2 19.0 %copy-start = (bf16[1024,256]{1,0:T(8,128)(2,1)S(1)}, bf16[1024,256]{1,0:T(8,128)(2,1)}, u32[]{:S(2)}) copy-start(bf16[1024,256]{1,0:T(8,128)(2,1)} %get-tuple-element.203.rows_ref) | copy-start | bytes 1572868
  169.2 19.0 %copy-start.3 = (bf16[256,256]{1,0:T(8,128)(2,1)S(1)}, bf16[256,256]{1,0:T(8,128)(2,1)}, u32[]{:S(2)}) copy-start(bf16[256,256]{1,0:T(8,128)(2,1)} %get-tuple-element.204.fresh_kept_ref) | copy-start | bytes 393220
  169.2 19.0 %copy-start.4 = (bf16[512,1024]{1,0:T(8,128)(2,1)S(1)}, bf16[512,1024]{1,0:T(8,128)(2,1)}, u32[]{:S(2)}) copy-start(bf16[512,1024]{1,0:T(8,128)(2,1)} %neighbour_counts.1.refs_1_.nbr_ref) | copy-start | bytes 3145732
  169.2 19.0 %copy-start.6 = (bf16[512,128]{1,0:T(8,128)(2,1)S(1)}, bf16[512,128]{1,0:T(8,128)(2,1)}, u32[]{:S(2)}) copy-start(bf16[512,128]{1,0:T(8,128)(2,1)} %codes.1.refs_2_.codes_ref) | copy-start | bytes 393220
  169.2 19.0 %copy-start.8 = (bf16[512,256]{1,0:T(8,128)(2,1)S(1)}, bf16[512,256]{1,0:T(8,128)(2,1)}, u32[]{:S(2)}) copy-start(bf16[512,256]{1,0:T(8,128)(2,1)} %w_out_ref.1) | copy-start | bytes 786436
  184.7 3.5 %collective-permute-start.7 = (bf16[512,256]{1,0:T(8,128)(2,1)S(1)}, bf16[512,256]{1,0:T(8,128)(2,1)S(1)}, u32[]{:S(2)}, u32[]{:S(2)}) collective-permute-start(bf16[512,256]{1,0:T(8,128)(2,1)S(1)} %bitcast.115), channel_id=1, source_target_pairs={{0,32},{32,0},{64,96},{96,64},{128,160},{160,128},{192,224},{224,1... | collective-permute-start | bytes 786440 | tf_op jit(solution)/shard_map/ppermute | solution.py:547

commit v3 on v2

--- a/solution.py
+++ b/solution.py
@@ -89,7 +89,7 @@
     low_out[...] = low
 
 
-def links_kernel(begin, after_ref, src_ref, dst_ref, gap_ref, count_ref, table_ref, w_code_ref, links_out, code_out, inv_out):
+def links_kernel(begin, after_ref, src_ref, dst_ref, gap_ref, count_ref, table_ref, w_code_ref, touched_ref, links_out, code_out, inv_out, free_out):
     turn = begin + pl.program_id(0)
     touch, slots = links_out.shape[1:]
     events = src_ref.shape[1]
@@ -99,6 +99,8 @@
     member_f = jnp.where(member_mask, 1.0, 0.0)
     member = member_f.astype(BF16)
     inv = 1.0 / jnp.sum(member_f, axis=1, keepdims=True)
+    hit = dot(pick_rows(free_out.shape[1], touched_ref[row, :]), jnp.ones((touch, 128), BF16))
+    free_out[0] = (1.0 - hit).astype(BF16)
     inv_out[0] = jnp.broadcast_to(inv, inv_out.shape[1:])
     dst_pick = pick_rows(slots, dst_ref[row, :])
     links_out[0] = dot_nt(member, dst_pick).astype(BF16)
@@ -121,11 +123,12 @@
     links_ref,
     code_ref,
     inv_ref,
+    free_ref,
     *rest,
 ):
     outs = rest[turn > 1 : (turn > 1) + 7]
     total_out, inv_out, links_out, base_out, gh_out, held_out, kept_out = outs
-    links_scr, code_scr, memory_scr, sems, snap_sem = rest[-5:]
+    links_scr, code_scr, free_scr, memory_scr, sems, snap_sem = rest[-6:]
     rows, touch, half = memory_ref.shape[0], touched_ref.shape[1], own_ref.shape[0]
     loads = copies(
         [
@@ -133,6 +136,7 @@
             (links_ref.at[at, :, half:], links_out),
             (code_ref.at[at], code_scr),
             (inv_ref.at[at], inv_out),
+            (free_ref.at[at], free_scr),
         ],
         sems,
     )
@@ -140,7 +144,7 @@
         copy.start()
     memory = memory_ref[...]
     if turn > 0:
-        snap_store = pltpu.make_async_copy(memory_scr, rest[-6], snap_sem)
+        snap_store = pltpu.make_async_copy(memory_scr, rest[-7], snap_sem)
 
         @pl.when(me_ref[0] == turn - 1)
         def _():
@@ -152,9 +156,8 @@
     held_out[...] = held
     gh_out[...] = dot(held, w_hid_ref[...])
     base = dot(held, w_msg_ref[:DM, :])
-    now = touched_ref[turn : turn + 1, :]
-    hit = dot(pick_rows(rows, now), jnp.ones((touch, 128), BF16))
-    free = (1.0 - hit).astype(BF16)
+    loads[4].wait()
+    free = free_scr[...]
     kept_out[...] = memory * jnp.concatenate([free, free], axis=1)
     loads[0].wait()
     total_out[...] = dot(links_scr[...], own_ref[...])
@@ -493,13 +496,15 @@
                 in_hbm((number, touch, slots), BF16),
                 in_hbm((number, touch, DM), BF16),
                 in_hbm((number, touch, 128), F32),
+                in_hbm((number, rows, 128), BF16),
             ),
-            [HBM] + [VMEM] * 3 + [SMEM] + [VMEM] * 2,
-            (*stay([after]), src_all, dst_all, gap_all, count_all, table, w_msg),
+            [HBM] + [VMEM] * 3 + [SMEM] + [VMEM] * 3,
+            (*stay([after]), src_all, dst_all, gap_all, count_all, table, w_msg, touched),
             out_specs=(
                 pl.BlockSpec((1, touch, slots), lambda t: (t, 0, 0)),
                 pl.BlockSpec((1, touch, DM), lambda t: (t, 0, 0)),
                 pl.BlockSpec((1, touch, 128), lambda t: (t, 0, 0)),
+                pl.BlockSpec((1, rows, 128), lambda t: (t, 0, 0)),
             ),
             grid=(number,),
         )
@@ -559,7 +564,7 @@
                 shape((rows, DM), BF16),
             )
             + (in_hbm((rows, DM), F32),) * (turn > 0),
-            [SMEM] + [VMEM] * 6 + [HBM] * (3 + len(snap)),
+            [SMEM] + [VMEM] * 6 + [HBM] * (4 + len(snap)),
             (
                 me_s,
                 own,
@@ -574,11 +579,12 @@
             scratch_shapes=[
                 pltpu.VMEM((touch, half), BF16),
                 pltpu.VMEM((touch, DM), BF16),
+                pltpu.VMEM((rows, 128), BF16),
                 pltpu.VMEM((rows, DM), F32),
-                pltpu.SemaphoreType.DMA((4,)),
+                pltpu.SemaphoreType.DMA((5,)),
                 pltpu.SemaphoreType.DMA,
             ],
-            input_output_aliases={10: 7} if snap else {},
+            input_output_aliases={11: 7} if snap else {},
         )
         ready, snap = outs[:7], outs[7:]
         if turn + 1 == sections:

time: 193 us -> 194 us (level)
  transfers between devices with their start and end apart: 11 -> 11, of which waited for: 2 -> 2; matrix products, arithmetic and copies ran while one was open for 2% -> 2% of each run, Pallas kernels for 16% -> 17%
where the time goes in v3:
time: 194 us
  blocking collectives  95.9 us (49%)
  Pallas kernels  48.8 us (25%)
  starting transfers between devices  37.3 us (19%)
  waiting for transfers between devices  5.26 us (3%)
  local copies, waits for them, and re-layouts  4.08 us (2%)
  between operations  1.99 us (1%)
    all_to_all x6, blocking collectives, body(): lax.all_to_all(served.reshape(shards, part, DM), 'node', split_axis=0, co...  95.9 us
    pallas_call x21, Pallas kernels, call(): pl.pallas_call(kernel, out_shape=outs, in_specs=ins, compiler_params=para...  46.3 us
    all_to_all x2, starting transfers between devices, body(): lax.all_to_all(served.reshape(shards, part, DM), 'node', split_axis=0, co...  15.6 us
    ppermute x8, starting transfers between devices, body(): other = lax.ppermute(own, 'tm', swap)  15.1 us
    all_to_all x1, starting transfers between devices, body(): lax.all_to_all(packed, 'tm', split_axis=0, concat_axis=0, tiled=True)  6.52 us
    all_to_all x2, waiting for transfers between devices, body(): lax.all_to_all(served.reshape(shards, part, DM), 'node', split_axis=0, co...  5.23 us
  transfers between devices with their start and end apart: 11, of which 2 were waited for; matrix products, arithmetic and copies ran while one was open for 2% of the time, Pallas kernels for 17%

profile of v3, /device:TPU:1, one launch (start us, length us, event | category | flops | bytes accessed | tf_op | source)
XLA Modules:
  0.0 193.5 jit_solution(14254216902319976304)
XLA Ops:
  2.8 6.5 %all-to-all-start = ((s32[8,24,128]{2,1,0:T(8,128)}), s32[8,24,128]{2,1,0:T(8,128)S(1)}, u32[]{:S(2)}, u32[]{:S(2)}) async-start(s32[8,24,128]{2,1,0:T(8,128)} %pack.1), calls=%async_computation | async-start | bytes 196608 | tf_op jit(solution)/shard_map/all_to_all | solution.py:435
  12.5 1.8 table.1
  16.1 10.5 %all-to-all-start.1 = ((bf16[32,16,256]{2,1,0:T(8,128)(2,1)}), bf16[32,16,256]{2,1,0:T(8,128)(2,1)S(1)}, u32[]{:S(2)}, u32[]{:S(2)}) async-start(bf16[32,16,256]{2,1,0:T(8,128)(2,1)} %bitcast.10), calls=%async_computation.1 | async-start | bytes 524288 | tf_op jit(solution)/shard_map/all_to_all | solution.py:520
  26.8 7.9 %links.2 = (bf16[6,256,1024]{2,1,0:T(8,128)(2,1)}, bf16[6,256,256]{2,1,0:T(8,128)(2,1)}, f32[6,256,128]{2,1,0:T(8,128)}, bf16[6,512,128]{2,1,0:T(8,128)(2,1)}) custom-call(f32[512,256]{1,0:T(8,128)} %after_ref.1, s32[8,512]{1,0:T(8,128)S(1)} %get-tuple-element.214.src_ref, s32[8,512]{1,0:T(8,128)S(1)} %get-tuple-element.213.dst_ref, ...), custom_call_target="tpu_custom_call" | custom-call | flops 1000000000 | bytes 4194304 | tf_op jit(solution)/shard_map/links/pallas_call | solution.py:464
  34.7 3.1 %all-to-all-done.1 = bf16[32,16,256]{2,1,0:T(8,128)(2,1)S(1)} async-done(((bf16[32,16,256]{2,1,0:T(8,128)(2,1)}), bf16[32,16,256]{2,1,0:T(8,128)(2,1)S(1)}, u32[]{:S(2)}, u32[]{:S(2)}) %all-to-all-start.1) | async-done | bytes 262176 | tf_op jit(solution)/shard_map/all_to_all | solution.py:520
  37.9 2.4 %collective-permute-start = (bf16[512,256]{1,0:T(8,128)(2,1)S(1)}, bf16[512,256]{1,0:T(8,128)(2,1)S(1)}, u32[]{:S(2)}, u32[]{:S(2)}) collective-permute-start(bf16[512,256]{1,0:T(8,128)(2,1)S(1)} %tie.2.own_ref), channel_id=1, source_target_pairs={{0,32},{32,0},{64,96},{96,64},{128,160},{160,128},{192,224},{224,1... | collective-permute-start | bytes 786440 | tf_op jit(solution)/shard_map/ppermute | solution.py:552
  40.3 2.0 %ready.8 = (f32[256,256]{1,0:T(8,128)S(1)}, f32[256,128]{1,0:T(8,128)S(1)}, bf16[256,512]{1,0:T(8,128)(2,1)S(1)}, f32[256,256]{1,0:T(8,128)S(1)}, f32[256,768]{1...) custom-call(s32[1]{0:T(128)} %bitcast.me_ref, bf16[512,256]{1,0:T(8,128)(2,1)S(1)} %tie.2.own_ref, ...), custom_call_target="tpu_custom_call" | custom-call | flops 1000000000 | bytes 4194304 | tf_op jit(solution)/shard_map/ready/pallas_call | solution.py:464
  42.3 2.0 %update.7 = (bf16[512,256]{1,0:T(8,128)(2,1)}, bf16[512,256]{1,0:T(8,128)(2,1)}, bf16[1024,256]{1,0:T(8,128)(2,1)}, bf16[256,256]{1,0:T(8,128)(2,1)}) custom-call(s32[1]{0:T(128)} %bitcast.me_ref, bf16[512,256]{1,0:T(8,128)(2,1)S(1)} %tie.2.own_ref, bf16[512,256]{1,0:T(8,128)(2,1)S(1)} %collective-permute-done.other_ref, ...), custom_call_target="tpu_custom_call" | custom-call | flops 1000000000 | bytes 4194304 | tf_op jit(solution)/shard_map/update/pallas_call | solution.py:464
  44.4 5.1 %all-to-all-start.2 = ((bf16[32,16,256]{2,1,0:T(8,128)(2,1)}), bf16[32,16,256]{2,1,0:T(8,128)(2,1)S(1)}, u32[]{:S(2)}, u32[]{:S(2)}) async-start(bf16[32,16,256]{2,1,0:T(8,128)(2,1)} %bitcast.12), calls=%async_computation.2 | async-start | bytes 524288 | tf_op jit(solution)/shard_map/all_to_all | solution.py:520
  49.7 3.5 %links.3 = (bf16[2,256,1024]{2,1,0:T(8,128)(2,1)}, bf16[2,256,256]{2,1,0:T(8,128)(2,1)}, f32[2,256,128]{2,1,0:T(8,128)}, bf16[2,512,128]{2,1,0:T(8,128)(2,1)}) custom-call(bf16[512,256]{1,0:T(8,128)(2,1)} %get-tuple-element.122.after_ref.memory_ref, s32[8,512]{1,0:T(8,128)S(1)} %get-tuple-element.214.src_ref, s32[8,512]{1,0:T(8,128)S(1)} %get-tuple-element.213.dst_ref, ...), custom_call_target="tpu_custom_call" | custom-call | flops 1000000000 | bytes 4194304 | tf_op jit(solution)/shard_map/links/pallas_call | solution.py:464
  53.2 2.6 %neighbour_counts.1.refs_1_.nbr_ref = bf16[512,1024]{1,0:T(8,128)(2,1)} custom-call(bf16[512,256]{1,0:T(8,128)(2,1)} %get-tuple-element.122.after_ref.memory_ref, s32[512,21]{1,0:T(8,128)S(1)} %bitcast.117), custom_call_target="tpu_custom_call" | custom-call | flops 1000000000 | bytes 4194304 | tf_op jit(solution)/shard_map/neighbour_counts/pallas_call | solution.py:464
  55.8 2.8 %codes.1.refs_2_.codes_ref = bf16[512,128]{1,0:T(8,128)(2,1)} custom-call(bf16[512,256]{1,0:T(8,128)(2,1)} %get-tuple-element.122.after_ref.memory_ref, s32[512,21]{1,0:T(8,128)S(1)} %bitcast.118, bf16[1024,128]{1,0:T(8,128)(2,1)S(1)} %get-tuple-element.107.rest_2_.table_ref.high_ref, bf16[1024,128]{1,0:T(8,128)(2,1)S(1)} %get-tuple-element.123.low_ref), custom_call_target="tpu_custom_call" | custom-call | flops 1000000000 | bytes 4194304 | tf_op jit(solution)/shard_map/codes/pallas_call | solution.py:464
  58.6 2.1 %all-to-all-done.2 = bf16[32,16,256]{2,1,0:T(8,128)(2,1)S(1)} async-done(((bf16[32,16,256]{2,1,0:T(8,128)(2,1)}), bf16[32,16,256]{2,1,0:T(8,128)(2,1)S(1)}, u32[]{:S(2)}, u32[]{:S(2)}) %all-to-all-start.2) | async-done | bytes 262176 | tf_op jit(solution)/shard_map/all_to_all | solution.py:520
  60.7 2.4 %collective-permute-start.1 = (bf16[512,256]{1,0:T(8,128)(2,1)S(1)}, bf16[512,256]{1,0:T(8,128)(2,1)S(1)}, u32[]{:S(2)}, u32[]{:S(2)}) collective-permute-start(bf16[512,256]{1,0:T(8,128)(2,1)S(1)} %tie.3.own_ref), channel_id=1, source_target_pairs={{0,32},{32,0},{64,96},{96,64},{128,160},{160,128},{192,224},{224,1... | collective-permute-start | bytes 786440 | tf_op jit(solution)/shard_map/ppermute | solution.py:552
  63.1 1.7 ready.9
  64.9 1.9 %update.8 = (bf16[512,256]{1,0:T(8,128)(2,1)S(1)}, bf16[512,256]{1,0:T(8,128)(2,1)S(1)}, bf16[1024,256]{1,0:T(8,128)(2,1)}, bf16[256,256]{1,0:T(8,128)(2,1)}) custom-call(s32[1]{0:T(128)} %bitcast.me_ref, bf16[512,256]{1,0:T(8,128)(2,1)S(1)} %tie.3.own_ref, ...), custom_call_target="tpu_custom_call", output_to_operand_aliasing={{2}: (14, {}), {3}: (15, {})} | custom-call | flops 1000000000 | bytes 4194304 | tf_op jit(solution)/shard_map/update/pallas_call | solution.py:464
  66.8 18.6 %all_to_all.45 = bf16[32,16,256]{2,1,0:T(8,128)(2,1)S(1)} all-to-all(bf16[32,16,256]{2,1,0:T(8,128)(2,1)S(1)} %bitcast.121), channel_id=1, replica_groups=mesh['tm'=8,'node'=32] {'node'}, dimensions={0} | all-to-all | bytes 524288 | tf_op jit(solution)/shard_map/all_to_all | solution.py:520
  86.0 1.9 ready.10
  89.2 16.0 %all_to_all.46 = bf16[32,16,256]{2,1,0:T(8,128)(2,1)S(1)} all-to-all(bf16[32,16,256]{2,1,0:T(8,128)(2,1)S(1)} %bitcast.122), channel_id=1, replica_groups=mesh['tm'=8,'node'=32] {'node'}, dimensions={0} | all-to-all | bytes 524288 | tf_op jit(solution)/shard_map/all_to_all | solution.py:520
  105.2 1.8 collective-permute-start.3
  110.0 15.3 %all_to_all.47 = bf16[32,16,256]{2,1,0:T(8,128)(2,1)S(1)} all-to-all(bf16[32,16,256]{2,1,0:T(8,128)(2,1)S(1)} %bitcast.123), channel_id=1, replica_groups=mesh['tm'=8,'node'=32] {'node'}, dimensions={0} | all-to-all | bytes 524288 | tf_op jit(solution)/shard_map/all_to_all | solution.py:520
  125.3 2.0 %collective-permute-start.4 = (bf16[512,256]{1,0:T(8,128)(2,1)S(1)}, bf16[512,256]{1,0:T(8,128)(2,1)S(1)}, u32[]{:S(2)}, u32[]{:S(2)}) collective-permute-start(bf16[512,256]{1,0:T(8,128)(2,1)S(1)} %bitcast.111), channel_id=1, source_target_pairs={{0,32},{32,0},{64,96},{96,64},{128,160},{160,128},{192,224},{224,1... | collective-permute-start | bytes 786440 | tf_op jit(solution)/shard_map/ppermute | solution.py:552
  127.3 1.7 ready.12
  130.3 15.3 %all_to_all.48 = bf16[32,16,256]{2,1,0:T(8,128)(2,1)S(1)} all-to-all(bf16[32,16,256]{2,1,0:T(8,128)(2,1)S(1)} %bitcast.124), channel_id=1, replica_groups=mesh['tm'=8,'node'=32] {'node'}, dimensions={0} | all-to-all | bytes 524288 | tf_op jit(solution)/shard_map/all_to_all | solution.py:520
  145.6 2.0 %collective-permute-start.5 = (bf16[512,256]{1,0:T(8,128)(2,1)S(1)}, bf16[512,256]{1,0:T(8,128)(2,1)S(1)}, u32[]{:S(2)}, u32[]{:S(2)}) collective-permute-start(bf16[512,256]{1,0:T(8,128)(2,1)S(1)} %bitcast.99), channel_id=1, source_target_pairs={{0,32},{32,0},{64,96},{96,64},{128,160},{160,128},{192,224},{224,1... | collective-permute-start | bytes 786440 | tf_op jit(solution)/shard_map/ppermute | solution.py:552
  147.5 1.7 ready.13
  150.6 15.3 %all_to_all.49 = bf16[32,16,256]{2,1,0:T(8,128)(2,1)S(1)} all-to-all(bf16[32,16,256]{2,1,0:T(8,128)(2,1)S(1)} %bitcast.125), channel_id=1, replica_groups=mesh['tm'=8,'node'=32] {'node'}, dimensions={0} | all-to-all | bytes 524288 | tf_op jit(solution)/shard_map/all_to_all | solution.py:520
  165.8 2.0 %collective-permute-start.6 = (bf16[512,256]{1,0:T(8,128)(2,1)S(1)}, bf16[512,256]{1,0:T(8,128)(2,1)S(1)}, u32[]{:S(2)}, u32[]{:S(2)}) collective-permute-start(bf16[512,256]{1,0:T(8,128)(2,1)S(1)} %bitcast.102), channel_id=1, source_target_pairs={{0,32},{32,0},{64,96},{96,64},{128,160},{160,128},{192,224},{224,1... | collective-permute-start | bytes 786440 | tf_op jit(solution)/shard_map/ppermute | solution.py:552
  170.9 15.4 %all_to_all.50 = bf16[32,16,256]{2,1,0:T(8,128)(2,1)S(1)} all-to-all(bf16[32,16,256]{2,1,0:T(8,128)(2,1)S(1)} %bitcast.120), channel_id=1, replica_groups=mesh['tm'=8,'node'=32] {'node'}, dimensions={0} | all-to-all | bytes 524288 | tf_op jit(solution)/shard_map/all_to_all | solution.py:520
  186.3 2.0 %collective-permute-start.7 = (bf16[512,256]{1,0:T(8,128)(2,1)S(1)}, bf16[512,256]{1,0:T(8,128)(2,1)S(1)}, u32[]{:S(2)}, u32[]{:S(2)}) collective-permute-start(bf16[512,256]{1,0:T(8,128)(2,1)S(1)} %bitcast.114), channel_id=1, source_target_pairs={{0,32},{32,0},{64,96},{96,64},{128,160},{160,128},{192,224},{224,1... | collective-permute-start | bytes 786440 | tf_op jit(solution)/shard_map/ppermute | solution.py:552
  188.3 1.7 ready.15
  190.1 3.2 %last.1 = (bf16[512,256]{1,0:T(8,128)(2,1)}, f32[512,256]{1,0:T(8,128)}) custom-call(s32[1]{0:T(128)} %bitcast.me_ref, s32[8]{0:T(128)S(1)} %slice_reduce_fusion.count_ref.counts_ref, bf16[512,256]{1,0:T(8,128)(2,1)S(1)} %bitcast.116, bf16[512,256]{1,0:T(8,128)(2,1)S(1)} %collective-permute-done.7.other_ref, ...), custom_call_target="tpu_custom_call", output_to_operand_aliasing={{1}: (21, {})} | custom-call | flops 1000000000 | bytes 4194304 | tf_op jit(solution)/shard_map/last/pallas_call | solution.py:464
  (63 shorter events, 17.2 us)
Async XLA Ops:
  0.6 14.5 %copy-start.5 = (f32[512,256]{1,0:T(8,128)S(1)}, f32[512,256]{1,0:T(8,128)}, u32[]{:S(2)}) copy-start(f32[512,256]{1,0:T(8,128)} %after_ref.1) | copy-start | bytes 1572868
  2.8 11.5 %all-to-all-start = ((s32[8,24,128]{2,1,0:T(8,128)}), s32[8,24,128]{2,1,0:T(8,128)S(1)}, u32[]{:S(2)}, u32[]{:S(2)}) async-start(s32[8,24,128]{2,1,0:T(8,128)} %pack.1), calls=%async_computation | async-start | bytes 196608 | tf_op jit(solution)/shard_map/all_to_all | solution.py:435
  16.1 21.7 %all-to-all-start.1 = ((bf16[32,16,256]{2,1,0:T(8,128)(2,1)}), bf16[32,16,256]{2,1,0:T(8,128)(2,1)S(1)}, u32[]{:S(2)}, u32[]{:S(2)}) async-start(bf16[32,16,256]{2,1,0:T(8,128)(2,1)} %bitcast.10), calls=%async_computation.1 | async-start | bytes 524288 | tf_op jit(solution)/shard_map/all_to_all | solution.py:520
  26.8 13.5 %copy-start.10 = (s32[1,1,10,512]{3,1,2,0:T(1,128)S(1)}, s32[1,1,10,512]{3,1,2,0:T(1,128)}, u32[]{:S(2)}) copy-start(s32[1,1,10,512]{3,1,2,0:T(1,128)} %param.24) | copy-start | bytes 61444
  26.8 13.5 %copy-start.1 = (bf16[256,768]{1,0:T(8,128)(2,1)S(1)}, bf16[256,768]{1,0:T(8,128)(2,1)}, u32[]{:S(2)}) copy-start(bf16[256,768]{1,0:T(8,128)(2,1)} %w_hid_ref.15) | copy-start | bytes 1179652
  37.9 4.4 %collective-permute-start = (bf16[512,256]{1,0:T(8,128)(2,1)S(1)}, bf16[512,256]{1,0:T(8,128)(2,1)S(1)}, u32[]{:S(2)}, u32[]{:S(2)}) collective-permute-start(bf16[512,256]{1,0:T(8,128)(2,1)S(1)} %tie.2.own_ref), channel_id=1, source_target_pairs={{0,32},{32,0},{64,96},{96,64},{128,160},{160,128},{192,224},{224,1... | collective-permute-start | bytes 786440 | tf_op jit(solution)/shard_map/ppermute | solution.py:552
  40.3 2.0 %copy-start.2 = (bf16[256,768]{1,0:T(8,128)(2,1)S(1)}, bf16[256,768]{1,0:T(8,128)(2,1)}, u32[]{:S(2)}) copy-start(bf16[256,768]{1,0:T(8,128)(2,1)} %w_in_ref.15) | copy-start | bytes 1179652
  42.3 7.2 %copy-start.11 = (s32[1,1,10,512]{3,1,2,0:T(1,128)S(1)}, s32[1,1,10,512]{3,1,2,0:T(1,128)}, u32[]{:S(2)}) copy-start(s32[1,1,10,512]{3,1,2,0:T(1,128)} %param.22) | copy-start | bytes 61444
  42.3 7.3 %copy-start.12 = (s32[1,1,512]{2,1,0:T(1,128)S(1)}, s32[1,1,512]{2,1,0:T(1,128)}, u32[]{:S(2)}) copy-start(s32[1,1,512]{2,1,0:T(1,128)} %param.18) | copy-start | bytes 6148
  44.4 16.3 %all-to-all-start.2 = ((bf16[32,16,256]{2,1,0:T(8,128)(2,1)}), bf16[32,16,256]{2,1,0:T(8,128)(2,1)S(1)}, u32[]{:S(2)}, u32[]{:S(2)}) async-start(bf16[32,16,256]{2,1,0:T(8,128)(2,1)} %bitcast.12), calls=%async_computation.2 | async-start | bytes 524288 | tf_op jit(solution)/shard_map/all_to_all | solution.py:520
  55.8 7.3 %copy-start.7 = (bf16[512,256]{1,0:T(8,128)(2,1)S(1)}, bf16[512,256]{1,0:T(8,128)(2,1)}, u32[]{:S(2)}) copy-start(bf16[512,256]{1,0:T(8,128)(2,1)} %get-tuple-element.122.after_ref.memory_ref) | copy-start | bytes 786436
  60.7 4.2 %collective-permute-start.1 = (bf16[512,256]{1,0:T(8,128)(2,1)S(1)}, bf16[512,256]{1,0:T(8,128)(2,1)S(1)}, u32[]{:S(2)}, u32[]{:S(2)}) collective-permute-start(bf16[512,256]{1,0:T(8,128)(2,1)S(1)} %tie.3.own_ref), channel_id=1, source_target_pairs={{0,32},{32,0},{64,96},{96,64},{128,160},{160,128},{192,224},{224,1... | collective-permute-start | bytes 786440 | tf_op jit(solution)/shard_map/ppermute | solution.py:552
  85.4 2.5 %collective-permute-start.2 = (bf16[512,256]{1,0:T(8,128)(2,1)S(1)}, bf16[512,256]{1,0:T(8,128)(2,1)S(1)}, u32[]{:S(2)}, u32[]{:S(2)}) collective-permute-start(bf16[512,256]{1,0:T(8,128)(2,1)S(1)} %bitcast.105), channel_id=1, source_target_pairs={{0,32},{32,0},{64,96},{96,64},{128,160},{160,128},{192,224},{224,1... | collective-permute-start | bytes 786440 | tf_op jit(solution)/shard_map/ppermute | solution.py:552
  105.2 3.6 %collective-permute-start.3 = (bf16[512,256]{1,0:T(8,128)(2,1)S(1)}, bf16[512,256]{1,0:T(8,128)(2,1)S(1)}, u32[]{:S(2)}, u32[]{:S(2)}) collective-permute-start(bf16[512,256]{1,0:T(8,128)(2,1)S(1)} %bitcast.108), channel_id=1, source_target_pairs={{0,32},{32,0},{64,96},{96,64},{128,160},{160,128},{192,224},{224,1... | collective-permute-start | bytes 786440 | tf_op jit(solution)/shard_map/ppermute | solution.py:552
  125.3 3.7 %collective-permute-start.4 = (bf16[512,256]{1,0:T(8,128)(2,1)S(1)}, bf16[512,256]{1,0:T(8,128)(2,1)S(1)}, u32[]{:S(2)}, u32[]{:S(2)}) collective-permute-start(bf16[512,256]{1,0:T(8,128)(2,1)S(1)} %bitcast.111), channel_id=1, source_target_pairs={{0,32},{32,0},{64,96},{96,64},{128,160},{160,128},{192,224},{224,1... | collective-permute-start | bytes 786440 | tf_op jit(solution)/shard_map/ppermute | solution.py:552
  145.6 3.7 %collective-permute-start.5 = (bf16[512,256]{1,0:T(8,128)(2,1)S(1)}, bf16[512,256]{1,0:T(8,128)(2,1)S(1)}, u32[]{:S(2)}, u32[]{:S(2)}) collective-permute-start(bf16[512,256]{1,0:T(8,128)(2,1)S(1)} %bitcast.99), channel_id=1, source_target_pairs={{0,32},{32,0},{64,96},{96,64},{128,160},{160,128},{192,224},{224,1... | collective-permute-start | bytes 786440 | tf_op jit(solution)/shard_map/ppermute | solution.py:552
  165.8 3.7 %collective-permute-start.6 = (bf16[512,256]{1,0:T(8,128)(2,1)S(1)}, bf16[512,256]{1,0:T(8,128)(2,1)S(1)}, u32[]{:S(2)}, u32[]{:S(2)}) collective-permute-start(bf16[512,256]{1,0:T(8,128)(2,1)S(1)} %bitcast.102), channel_id=1, source_target_pairs={{0,32},{32,0},{64,96},{96,64},{128,160},{160,128},{192,224},{224,1... | collective-permute-start | bytes 786440 | tf_op jit(solution)/shard_map/ppermute | solution.py:552
  169.5 18.7 %copy-start.9 = (bf16[356,256]{1,0:T(8,128)(2,1)S(1)}, bf16[356,256]{1,0:T(8,128)(2,1)}, u32[]{:S(2)}) copy-start(bf16[356,256]{1,0:T(8,128)(2,1)} %param.30) | copy-start | bytes 546820
  170.8 19.2 %copy-start = (bf16[1024,256]{1,0:T(8,128)(2,1)S(1)}, bf16[1024,256]{1,0:T(8,128)(2,1)}, u32[]{:S(2)}) copy-start(bf16[1024,256]{1,0:T(8,128)(2,1)} %get-tuple-element.207.rows_ref) | copy-start | bytes 1572868
  170.9 19.2 %copy-start.3 = (bf16[256,256]{1,0:T(8,128)(2,1)S(1)}, bf16[256,256]{1,0:T(8,128)(2,1)}, u32[]{:S(2)}) copy-start(bf16[256,256]{1,0:T(8,128)(2,1)} %get-tuple-element.208.fresh_kept_ref) | copy-start | bytes 393220
  170.9 19.2 %copy-start.4 = (bf16[512,1024]{1,0:T(8,128)(2,1)S(1)}, bf16[512,1024]{1,0:T(8,128)(2,1)}, u32[]{:S(2)}) copy-start(bf16[512,1024]{1,0:T(8,128)(2,1)} %neighbour_counts.1.refs_1_.nbr_ref) | copy-start | bytes 3145732
  170.9 19.2 %copy-start.6 = (bf16[512,128]{1,0:T(8,128)(2,1)S(1)}, bf16[512,128]{1,0:T(8,128)(2,1)}, u32[]{:S(2)}) copy-start(bf16[512,128]{1,0:T(8,128)(2,1)} %codes.1.refs_2_.codes_ref) | copy-start | bytes 393220
  170.9 19.2 %copy-start.8 = (bf16[512,256]{1,0:T(8,128)(2,1)S(1)}, bf16[512,256]{1,0:T(8,128)(2,1)}, u32[]{:S(2)}) copy-start(bf16[512,256]{1,0:T(8,128)(2,1)} %w_out_ref.1) | copy-start | bytes 786436
  186.3 3.7 %collective-permute-start.7 = (bf16[512,256]{1,0:T(8,128)(2,1)S(1)}, bf16[512,256]{1,0:T(8,128)(2,1)S(1)}, u32[]{:S(2)}, u32[]{:S(2)}) collective-permute-start(bf16[512,256]{1,0:T(8,128)(2,1)S(1)} %bitcast.114), channel_id=1, source_target_pairs={{0,32},{32,0},{64,96},{96,64},{128,160},{160,128},{192,224},{224,1... | collective-permute-start | bytes 786440 | tf_op jit(solution)/shard_map/ppermute | solution.py:552
